TPU v7x, 128 devices: a whole 4x4x4 slice. The times are simulated.
128 devices in a mesh: row: 8 (over z_hi, x), col: 8 (over y, core), rep: 2 (over z_lo).
Axes of the slice: x: 4, y: 4, z: 4 (z_hi: 2, z_lo: 2; z = z_hi * 2 + z_lo), core: 2. Of those that a mesh axis runs over, the one named last changes fastest.
Arguments:
- latents: bfloat16 [2048, 6144], P('col', ('row', 'rep')), may hold values from -6 to 6
- probe: int32 [2048, 6144], P(None, ('row', 'rep')), may hold values from 0 to 1
- w_gate: bfloat16 [6144, 16384], P(('row', 'rep'), 'col'), may hold values from -0.078125 to 0.078125
- w_up: bfloat16 [6144, 16384], P(('row', 'rep'), 'col'), may hold values from -0.078125 to 0.078125
- w_down: bfloat16 [16384, 6144], P('col', ('row', 'rep')), may hold values from -0.046875 to 0.046875
Outputs:
- grad_in: bfloat16 [2048, 6144], P('col', ('row', 'rep'))
All inputs are finite; a program needn't handle non-finite values.
Results may differ from a plain program's by a relative error of at most 0.0049.
Values may be sent and summed in bfloat16 or wider, within the bound.
No kernel may reach another device: no remote copies, remote signals or barrier semaphores. Data moves between devices by JAX's collectives and lax.ppermute only.
A program may use at most 256 MiB of HBM per device.

v0:
```python
import jax
import jax.numpy as jnp
from jax import lax
from jax.sharding import PartitionSpec as P


def shards(latents, probe, w_gate, w_up, w_down):
    panel = lax.all_gather(latents, "col", axis=0, tiled=True)
    signs = (2 * probe - 1).astype(jnp.bfloat16)
    contract = (((1,), (1,)), ((), ()))
    gate_term = jnp.dot(panel, w_gate, preferred_element_type=jnp.float32)
    up_term = jnp.dot(panel, w_up, preferred_element_type=jnp.float32)
    back_term = lax.dot_general(signs, w_down, contract, preferred_element_type=jnp.float32)
    sums = lax.psum_scatter(
        jnp.concatenate((gate_term, up_term, back_term), axis=1),
        ("row", "rep"),
        scatter_dimension=0,
        tiled=True,
    )
    width = w_gate.shape[1]
    gate = sums[:, :width]
    back = sums[:, 2 * width :]
    sigma = jax.nn.sigmoid(gate)
    gate_slope = (back * sums[:, width : 2 * width] * sigma * (1.0 + gate * (1.0 - sigma))).astype(
        jnp.bfloat16
    )
    up_slope = (back * gate * sigma).astype(jnp.bfloat16)
    gate_slope, up_slope = (gate_slope, up_slope)
    gate_all, up_all = (
        lax.all_gather(gate_slope, ("row", "rep"), axis=0, tiled=True),
        lax.all_gather(up_slope, ("row", "rep"), axis=0, tiled=True),
    )
    total = lax.dot_general(gate_all, w_gate, contract, preferred_element_type=jnp.float32)
    result = lax.psum_scatter(
        total + lax.dot_general(up_all, w_up, contract, preferred_element_type=jnp.float32),
        "col",
        scatter_dimension=0,
        tiled=True,
    )
    return result.astype(jnp.bfloat16)


def solution(mesh):
    in_specs = (
        P("col", ("row", "rep")),
        P(None, ("row", "rep")),
        P(("row", "rep"), "col"),
        P(("row", "rep"), "col"),
        P("col", ("row", "rep")),
    )
    out_specs = P("col", ("row", "rep"))
    return jax.shard_map(shards, mesh=mesh, in_specs=in_specs, out_specs=out_specs, check_vma=False)
```

profile of v0, /device:TPU:24, one launch (start us, length us, event | category | flops | bytes accessed | tf_op | source)
XLA Modules:
  0.0 1547.3 jit_solution(6300711802983840832)
XLA Ops:
  6.5 0.0 copy-start
  6.5 0.0 all-gather.4.cloned.1.call-start
  6.5 0.7 all-gather.4.cloned.1.call-update
  7.3 0.0 copy-start.2
  7.3 0.0 reduce-scatter.3.cloned.1.call-start
  7.3 12.7 fusion
  20.1 13.9 all-gather.4.cloned.1.call-done
  34.0 0.0 copy-done.2
  34.0 0.0 copy-start.1
  34.0 9.7 fusion.9
  43.7 0.0 copy-done
  43.7 0.0 copy-done.1
  43.7 8.2 fusion.8
  52.0 34.8 %pad_maximum_fusion = f32[2048,6144]{0,1:T(8,128)} fusion(f32[2048,2048]{0,1:T(8,128)} %fusion, f32[2048,2048]{0,1:T(8,128)} %fusion.9, f32[2048,2048]{0,1:T(8,128)} %fusion.8), kind=kLoop, calls=%fused_computation | loop fusion | flops 25165824 | bytes 100663296 | tf_op jit(solution)/shard_map/concatenate | solution.py:15
  86.7 0.0 reduce-scatter.3.cloned.1.call-update
  86.7 0.0 all-gather.6.cloned.1.call-start
  86.8 1023.2 %reduce-scatter.3.cloned.1.call-done = f32[128,6144]{0,1:T(8,128)} async-done(((f32[2048,6144]{0,1:T(8,128)}), f32[128,6144]{0,1:T(8,128)}) %reduce-scatter.3.cloned.1.call-update) | async-done | bytes 3145744 | tf_op jit(solution)/shard_map/reduce_scatter | solution.py:14
  1110.0 3.3 multiply_convert_fusion
  1113.3 0.0 all-gather.6.cloned.1.call-update
  1113.4 0.0 all-gather.8.cloned.1.call-start
  1113.4 0.5 all-gather.8.cloned.1.call-update
  1113.9 0.2 reduce-scatter.5.cloned.1.call-start
  1114.2 177.7 %all-gather.6.cloned.1.call-done = bf16[2048,2048]{0,1:T(8,128)(2,1)} async-done(((bf16[128,2048]{0,1:T(8,128)(2,1)}), bf16[2048,2048]{0,1:T(8,128)(2,1)}) %all-gather.6.cloned.1.call-update) | async-done | bytes 8388624 | tf_op jit(solution)/shard_map/all_gather | solution.py:30
  1291.9 8.6 fusion.10
  1300.5 182.0 %all-gather.8.cloned.1.call-done = bf16[2048,2048]{0,1:T(8,128)(2,1)} async-done(((bf16[128,2048]{0,1:T(8,128)(2,1)}), bf16[2048,2048]{0,1:T(8,128)(2,1)}) %all-gather.8.cloned.1.call-update) | async-done | bytes 8388624 | tf_op jit(solution)/shard_map/all_gather | solution.py:31
  1482.5 10.4 convolution_add_fusion
  1492.9 0.0 reduce-scatter.5.cloned.1.call-update
  1492.9 46.1 %reduce-scatter.5.cloned.1.call-done = f32[256,384]{1,0:T(8,128)} async-done(((f32[2048,384]{1,0:T(8,128)}), f32[256,384]{1,0:T(8,128)}) %reduce-scatter.5.cloned.1.call-update) | async-done | bytes 393232 | tf_op jit(solution)/shard_map/reduce_scatter | solution.py:34
  1539.0 1.7 convert_element_type.15
Async XLA Ops:
  6.5 37.2 %copy-start = (bf16[384,2048]{1,0:T(8,128)(2,1)S(1)}, bf16[384,2048]{1,0:T(8,128)(2,1)}, u32[]{:S(2)}) copy-start(bf16[384,2048]{1,0:T(8,128)(2,1)} %param.7) | copy-start | bytes 4718596
  6.5 27.5 %all-gather.4.cloned.1.call-start = ((), (), s32[]{:S(2)}) async-start(), calls=%async_computation.2 | async-start | bytes 1769472 | tf_op jit(solution)/shard_map/all_gather | solution.py:8
  7.3 26.7 %copy-start.2 = (bf16[384,2048]{1,0:T(8,128)(2,1)S(1)}, bf16[384,2048]{1,0:T(8,128)(2,1)}, u32[]{:S(2)}) copy-start(bf16[384,2048]{1,0:T(8,128)(2,1)} %param.8) | copy-start | bytes 4718596
  7.3 1102.7 %reduce-scatter.3.cloned.1.call-start = ((), (), s32[]{:S(2)}) async-start(), calls=%async_computation.3 | async-start | bytes 53477376 | tf_op jit(solution)/shard_map/reduce_scatter | solution.py:14
  34.0 9.7 copy-start.1
  86.7 1205.2 %all-gather.6.cloned.1.call-start = ((), (), s32[]{:S(2)}) async-start(), calls=%async_computation.4 | async-start | bytes 8912896 | tf_op jit(solution)/shard_map/all_gather | solution.py:30
  1113.4 369.1 %all-gather.8.cloned.1.call-start = ((), (), s32[]{:S(2)}) async-start(), calls=%async_computation.5 | async-start | bytes 8912896 | tf_op jit(solution)/shard_map/all_gather | solution.py:31
  1113.9 425.1 %reduce-scatter.5.cloned.1.call-start = ((), (), s32[]{:S(2)}) async-start(), calls=%async_computation.6 | async-start | bytes 3538944 | tf_op jit(solution)/shard_map/reduce_scatter | solution.py:34
Sparse Core Ops, SparseCore 0:
  9.0 24.9 all-gather.3
  86.9 1023.1 reduce-scatter.2
  1113.5 178.3 all-gather.5
  1293.3 189.1 all-gather.7
  1493.0 45.9 reduce-scatter.4
where the time goes:
time: 1550 us
  waiting for transfers between devices  1440 us (93%)
  matrix products  49.7 us (3%)
  other arithmetic  39.8 us (3%)
    reduce_scatter x1, waiting for transfers between devices, shards(): lax.psum_scatter(jnp.concatenate((gate_term, up_term, back_term), axis=1)...  1020 us
    all_gather x1, waiting for transfers between devices, shards(): lax.all_gather(up_slope, ('row', 'rep'), axis=0, tiled=True)  182 us
    all_gather x1, waiting for transfers between devices, shards(): lax.all_gather(gate_slope, ('row', 'rep'), axis=0, tiled=True)  178 us
    reduce_scatter x1, waiting for transfers between devices, shards(): lax.psum_scatter(total + lax.dot_general(up_all, w_up, contract, preferre...  46.1 us
    concatenate x1, other arithmetic, shards(): jnp.concatenate((gate_term, up_term, back_term), axis=1)  34.8 us
  transfers between devices with their start and end apart: 5, of which 5 were waited for; matrix products, arithmetic and copies ran while one was open for 1% of the time, Pallas kernels for 0%

commit v1 on v0

v1 whole, which is shorter than its diff:
```python
import jax
import jax.numpy as jnp
from jax import lax
from jax.sharding import PartitionSpec as P

AXES = ("row", "col", "rep")
SIDE = 4
CHUNKS = ((3, 1), (2, 0))


def place(x, y, z, c):
    return (((z // 2) * SIDE + x) * 2 * SIDE + y * 2 + c) * 2 + z % 2


def pairs(move):
    found = []
    for x in range(SIDE):
        for y in range(SIDE):
            for z in range(SIDE):
                for c in range(2):
                    nx, ny, nz, nc = move(x, y, z, c)
                    found.append((place(x, y, z, c), place(nx % SIDE, ny % SIDE, nz % SIDE, nc)))
    return found


def along(axis, by):
    def move(x, y, z, c):
        step = by if c == 0 else -by
        return (x + step * (axis == "x"), y + step * (axis == "y"), z + step * (axis == "z"), c)

    return pairs(move)


AHEAD = {axis: along(axis, 1) for axis in "xyz"}
BEHIND = {axis: along(axis, -1) for axis in "xyz"}
ACROSS = along("z", 2)
CORES = pairs(lambda x, y, z, c: (x, y, z, 1 - c))


def send(value, route):
    return lax.ppermute(value, AXES, route)


def ring_gather(value, axis):
    near = send(value, AHEAD[axis])
    far = send(near, AHEAD[axis])
    return near, send(value, BEHIND[axis]), far


def shards(latents, probe, w_gate, w_up, w_down):
    f32, bf16 = jnp.float32, jnp.bfloat16
    row, col = lax.axis_index("row"), lax.axis_index("col")
    x, z = row % SIDE, (row // SIDE) * 2 + lax.axis_index("rep")
    core = col % 2
    even = core == 0
    s = 1 - 2 * core
    tokens, features = latents.shape
    hidden = w_gate.shape[1] // SIDE
    part = tokens // SIDE

    def ordered(own, near, next_, far, axis):
        return jnp.concatenate(
            (own, jnp.where(even, near, next_), jnp.where(even, next_, near), far), axis=axis
        )

    bits = lax.dynamic_slice_in_dim(probe, col * tokens, tokens, axis=0)
    rows = jnp.stack((latents, (2 * bits - 1).astype(bf16)))
    rows = ordered(rows, *ring_gather(rows, "z"), axis=2)

    def swap_z(piece):
        return (
            piece(z),
            send(piece((z + s) % SIDE), AHEAD["z"]),
            send(piece((z - s) % SIDE), BEHIND["z"]),
            send(piece((z + 2) % SIDE), ACROSS),
        )

    def gate_up_piece(i):
        return jnp.concatenate(
            [lax.dynamic_slice_in_dim(w, i * hidden, hidden, axis=1) for w in (w_gate, w_up)], axis=1
        )

    gate_up = ordered(*swap_z(gate_up_piece), axis=0)
    down = ordered(*swap_z(lambda i: lax.dynamic_slice_in_dim(w_down, i * hidden, hidden, axis=0)), axis=1)
    both = jnp.concatenate((gate_up, send(gate_up, CORES)), axis=1)

    slots = [rows, *ring_gather(rows, "y")]
    slots = [(mine, send(mine, CORES)) for mine in slots]

    totals = {}
    for chunk in CHUNKS:

        def block(kind, i):
            return jnp.concatenate(
                [
                    lax.dynamic_slice_in_dim(slots[slot][p][kind], i * part, part, axis=0)
                    for p in range(2)
                    for slot in chunk
                ],
                axis=0,
            )

        def reduced(term):
            relay = send(term((x + 2) % SIDE).astype(bf16), AHEAD["x"])
            ahead = send((term((x + s) % SIDE) + relay).astype(bf16), AHEAD["x"])
            behind = send(term((x - s) % SIDE).astype(bf16), BEHIND["x"])
            return term(x) + ahead + behind

        gate_up_sum = reduced(lambda i: jnp.dot(block(0, i), gate_up, preferred_element_type=f32))
        back = reduced(
            lambda i: lax.dot_general(
                block(1, i), down, (((1,), (1,)), ((), ())), preferred_element_type=f32
            )
        )
        gate, up = gate_up_sum[:, :hidden], gate_up_sum[:, hidden:]
        sigma = jax.nn.sigmoid(gate)
        slopes = jnp.concatenate(
            (
                (back * up * sigma * (1.0 + gate * (1.0 - sigma))).astype(bf16),
                (back * gate * sigma).astype(bf16),
            ),
            axis=1,
        )
        half = slopes.shape[0] // 2
        slopes = jnp.concatenate((slopes[:half], send(slopes[half:], CORES)), axis=1)
        gathered = jnp.concatenate((slopes, *ring_gather(slopes, "x")), axis=0)
        out = lax.dot_general(gathered, both, (((1,), (1,)), ((), ())), preferred_element_type=f32)
        out = out.reshape(SIDE, len(chunk), part, -1)
        for n, slot in enumerate(chunk):
            totals[slot] = out[:, n]

    relay = send(totals[3].astype(bf16), BEHIND["y"])
    near = send((totals[1] + relay).astype(bf16), BEHIND["y"])
    total = totals[0] + near + send(totals[2].astype(bf16), AHEAD["y"])
    own, low, high, far = (total[:, :, n * features : (n + 1) * features] for n in range(SIDE))
    relay = send(far, AHEAD["z"])
    near = send(jnp.where(even, high, low) + relay, AHEAD["z"])
    total = own + near + send(jnp.where(even, low, high), BEHIND["z"])
    total = total.astype(bf16)

    where = [jnp.int32(0), 1 + (s + 1) // 2, jnp.int32(3), 1 + (1 - s) // 2]
    where = jnp.stack(where)
    return jnp.concatenate(
        [lax.dynamic_index_in_dim(total, where[(j - x) % SIDE], 0, keepdims=False) for j in range(SIDE)],
        axis=0,
    )


def solution(mesh):
    in_specs = (
        P("col", ("row", "rep")),
        P(None, ("row", "rep")),
        P(("row", "rep"), "col"),
        P(("row", "rep"), "col"),
        P("col", ("row", "rep")),
    )
    out_specs = P("col", ("row", "rep"))
    return jax.shard_map(shards, mesh=mesh, in_specs=in_specs, out_specs=out_specs, check_vma=False)
```

time: 1550 us -> 259 us (0.17)
  waiting for transfers between devices: 1440 us -> 133 us
  starting transfers between devices: 0.34 us -> 75 us
  matrix products: 49.7 us -> 20.3 us
  other arithmetic: 39.8 us -> 11.5 us
    reduce_scatter x2 -> x0, waiting for transfers between devices: 1070 us -> none  [the longest x1 1020 us: shards(): lax.psum_scatter(jnp.concatenate((gate_term, up_term, back_term), axis=1)...]
    all_gather x3 -> x0, waiting for transfers between devices: 374 us -> none  [the longest x1 182 us: shards(): lax.all_gather(up_slope, ('row', 'rep'), axis=0, tiled=True)]
    ppermute x0 -> x43, waiting for transfers between devices: none -> 133 us  [send(): return lax.ppermute(value, AXES, route)]
    ppermute x0 -> x43, starting transfers between devices: none -> 75 us  [send(): return lax.ppermute(value, AXES, route)]
    concatenate x1 -> x10, other arithmetic: 34.8 us -> 4.4 us  [the longest x2 3.27 us: ordered(): jnp.concatenate((own, jnp.where(even, near, next_), jnp.where(even, next_...]
    dot_general x5 -> x18, matrix products: 49.7 us -> 20.3 us  [the longest x8 8.17 us: shards(): jnp.dot(block(0, i), gate_up, preferred_element_type=f32)]
  transfers between devices with their start and end apart: 5 -> 43, of which waited for: 5 -> 23; matrix products, arithmetic and copies ran while one was open for 1% -> 13% of each run, Pallas kernels for 0% -> 0%
where the time goes in v1:
time: 259 us; the launch traced here: 255 us
  waiting for transfers between devices  133 us (51%)
  starting transfers between devices  75 us (29%)
  matrix products  20.3 us (8%)
  other arithmetic  11.5 us (4%)
  between operations  8.23 us (3%)
  local copies, waits for them, and re-layouts  6.61 us (3%)
    ppermute x43, waiting for transfers between devices, send(): return lax.ppermute(value, AXES, route)  133 us
    ppermute x43, starting transfers between devices, send(): return lax.ppermute(value, AXES, route)  75 us
    dot_general x8, matrix products, shards(): jnp.dot(block(0, i), gate_up, preferred_element_type=f32)  8.17 us
    dot_general x2, matrix products, shards(): lax.dot_general(gathered, both, (((1,), (1,)), ((), ())), preferred_eleme...  6.91 us
    dot_general x8, matrix products, shards(): lax.dot_general(block(1, i), down, (((1,), (1,)), ((), ())), preferred_el...  5.25 us
  transfers between devices with their start and end apart: 43, of which 23 were waited for; matrix products, arithmetic and copies ran while one was open for 13% of the time, Pallas kernels for 0%

profile of v1, /device:TPU:24, one launch (start us, length us, event | category | flops | bytes accessed | tf_op | source)
XLA Modules:
  0.0 255.1 jit_solution(11317160172206015977)
XLA Ops:
  0.0 1.0 fusion.156
  1.0 1.7 pad_maximum_fusion.9
  2.8 4.0 %collective-permute-start.1 = (bf16[2,256,384]{2,1,0:T(8,128)(2,1)}, bf16[2,256,384]{2,1,0:T(8,128)(2,1)}, u32[]{:S(2)}, u32[]{:S(2)}) collective-permute-start(bf16[2,256,384]{2,1,0:T(8,128)(2,1)} %pad_maximum_fusion.9), channel_id=1, source_target_pairs={{0,65},{2,3},{1,0},{3,66},{64,1},{66,67},{65,64},{67,2},{4,69},{6,... | collective-permute-start | bytes 1179656 | tf_op jit(solution)/shard_map/ppermute | solution.py:41
  6.8 2.7 %constant_dynamic-slice_fusion.11 = (bf16[512,384]{1,0:T(8,128)(2,1)}, bf16[512,384]{1,0:T(8,128)(2,1)}, bf16[512,384]{1,0:T(8,128)(2,1)}, bf16[512,384]{1,0:T(8,128)(2,1)}) fusion(bf16[2048,384]{1,0:T(8,128)(2,1)} %param.9, s32[]{:T(128)S(6)} %select_n.261, s32[]{:T(128)S(6)} %select_n.264, s32[]{:T(128)S(6)} %select_n.270, s32[]{:T(128)S(6)} %select_n.266), kind=kLoop, calls=%fused_computation.289 | loop fusion | bytes 3145744 | tf_op jit(solution)/shard_map/dynamic_slice | solution.py:84
  9.5 3.2 %collective-permute-start.7 = (bf16[512,384]{1,0:T(8,128)(2,1)}, bf16[512,384]{1,0:T(8,128)(2,1)}, u32[]{:S(2)}, u32[]{:S(2)}) collective-permute-start(bf16[512,384]{1,0:T(8,128)(2,1)} %get-tuple-element.40), channel_id=1, source_target_pairs={{0,65},{2,3},{1,0},{3,66},{64,1},{66,67},{65,64},{67,2},{4,69},{6,... | collective-permute-start | bytes 1179656 | tf_op jit(solution)/shard_map/ppermute | solution.py:41
  13.3 2.1 collective-permute-start.13
  15.4 2.3 collective-permute-done
  18.0 1.2 collective-permute-start.12
  19.2 1.2 broadcast_select_fusion.5
  20.4 14.1 %collective-permute-done.2 = bf16[2,256,384]{2,1,0:T(8,128)(2,1)S(1)} collective-permute-done((bf16[2,256,384]{2,1,0:T(8,128)(2,1)}, bf16[2,256,384]{2,1,0:T(8,128)(2,1)S(1)}, u32[]{:S(2)}, u32[]{:S(2)}) %collective-permute-start.2) | collective-permute-done | bytes 393248 | tf_op jit(solution)/shard_map/ppermute | solution.py:41
  34.5 1.3 collective-permute-start.14
  36.3 1.8 collective-permute-start.3
  38.1 1.2 broadcast_select_fusion.3
  39.3 5.3 %collective-permute-done.13 = bf16[384,1024]{1,0:T(8,128)(2,1)} collective-permute-done((bf16[384,1024]{1,0:T(8,128)(2,1)S(1)}, bf16[384,1024]{1,0:T(8,128)(2,1)}, u32[]{:S(2)}, u32[]{:S(2)}) %collective-permute-start.13) | collective-permute-done | bytes 786464 | tf_op jit(solution)/shard_map/ppermute | solution.py:41
  44.6 5.7 %collective-permute-done.12 = bf16[384,1024]{1,0:T(8,128)(2,1)S(1)} collective-permute-done((bf16[384,1024]{1,0:T(8,128)(2,1)S(1)}, bf16[384,1024]{1,0:T(8,128)(2,1)S(1)}, u32[]{:S(2)}, u32[]{:S(2)}) %collective-permute-start.12) | collective-permute-done | bytes 786464 | tf_op jit(solution)/shard_map/ppermute | solution.py:41
  50.3 20.0 %collective-permute-start.5 = (bf16[2,256,1536]{2,1,0:T(8,128)(2,1)S(1)}, bf16[2,256,1536]{2,1,0:T(8,128)(2,1)S(1)}, u32[]{:S(2)}, u32[]{:S(2)}) collective-permute-start(bf16[2,256,1536]{2,1,0:T(8,128)(2,1)S(1)} %pad_maximum_fusion.2), channel_id=1, source_target_pairs={{0,2},{2,0},{1,3},{3,1},{64,66},{66,64},{65,67},{67,65},{4,6},{6,4... | collective-permute-start | bytes 4718600 | tf_op jit(solution)/shard_map/ppermute | solution.py:41
  70.3 1.2 broadcast_select_fusion.1
  71.6 3.1 %pad_maximum_fusion.1 = bf16[1536,1024]{1,0:T(8,128)(2,1)S(1)} fusion(bf16[384,1024]{1,0:T(8,128)(2,1)S(1)} %collective-permute-done.14, bf16[384,1024]{1,0:T(8,128)(2,1)S(1)} %get-tuple-element.36, bf16[384,1024]{1,0:T(8,128)(2,1)S(1)} %get-tuple-element.35, bf16[384,512]{1,0:T(8,128)(2,1)S(1)} %get-tuple-element.31, bf16[384,512]{1,0:T(8,128)(2,1)S(1)} %get-tuple-element.124), kind=kLoop, calls=%fused_computation.1 | loop fusion | flops 15728640 | bytes 6291456 | tf_op jit(solution)/shard_map/concatenate | solution.py:62
  76.5 8.5 %collective-permute-done.4 = bf16[2,256,1536]{2,1,0:T(8,128)(2,1)S(1)} collective-permute-done((bf16[2,256,1536]{2,1,0:T(8,128)(2,1)S(1)}, bf16[2,256,1536]{2,1,0:T(8,128)(2,1)S(1)}, u32[]{:S(2)}, u32[]{:S(2)}) %collective-permute-start.4) | collective-permute-done | bytes 1572896 | tf_op jit(solution)/shard_map/ppermute | solution.py:41
  85.2 0.8 copy-done.3
  86.7 1.6 collective-permute-start.9
  88.3 1.0 convolution_convert_fusion.3
  89.4 1.8 collective-permute-start.15
  91.2 1.0 convolution_convert_fusion.2
  92.2 4.3 %collective-permute-done.24 = bf16[2,256,1536]{2,1,0:T(8,128)(2,1)S(1)} collective-permute-done((bf16[2,256,1536]{2,1,0:T(8,128)(2,1)S(1)}, bf16[2,256,1536]{2,1,0:T(8,128)(2,1)S(1)}, u32[]{:S(2)}, u32[]{:S(2)}) %collective-permute-start.24) | collective-permute-done | bytes 1572896 | tf_op jit(solution)/shard_map/ppermute | solution.py:41
  96.6 2.8 %collective-permute-start.17 = (bf16[256,1024]{1,0:T(8,128)(2,1)S(1)}, bf16[256,1024]{1,0:T(8,128)(2,1)S(1)}, u32[]{:S(2)}, u32[]{:S(2)}) collective-permute-start(bf16[256,1024]{1,0:T(8,128)(2,1)S(1)} %convolution_convert_fusion.2), channel_id=1, source_target_pairs={{0,48},{2,18},{1,49},{3,19},{64,112},{66,82},{65,113},{67,83},{4,5... | collective-permute-start | bytes 1572872 | tf_op jit(solution)/shard_map/ppermute | solution.py:41
  100.1 1.0 fusion.26
  102.1 3.0 %collective-permute-start.11 = (bf16[256,512]{1,0:T(8,128)(2,1)S(1)}, bf16[256,512]{1,0:T(8,128)(2,1)S(1)}, u32[]{:S(2)}, u32[]{:S(2)}) collective-permute-start(bf16[256,512]{1,0:T(8,128)(2,1)S(1)} %convolution_convert_fusion.6), channel_id=1, source_target_pairs={{0,48},{2,18},{1,49},{3,19},{64,112},{66,82},{65,113},{67,83},{4,5... | collective-permute-start | bytes 786440 | tf_op jit(solution)/shard_map/ppermute | solution.py:41
  105.7 3.4 %collective-permute-done.17 = bf16[256,1024]{1,0:T(8,128)(2,1)S(1)} collective-permute-done((bf16[256,1024]{1,0:T(8,128)(2,1)S(1)}, bf16[256,1024]{1,0:T(8,128)(2,1)S(1)}, u32[]{:S(2)}, u32[]{:S(2)}) %collective-permute-start.17) | collective-permute-done | bytes 524320 | tf_op jit(solution)/shard_map/ppermute | solution.py:41
  109.1 6.1 %collective-permute-done.16 = bf16[256,1024]{1,0:T(8,128)(2,1)S(1)} collective-permute-done((bf16[256,1024]{1,0:T(8,128)(2,1)S(1)}, bf16[256,1024]{1,0:T(8,128)(2,1)S(1)}, u32[]{:S(2)}, u32[]{:S(2)}) %collective-permute-start.16) | collective-permute-done | bytes 524320 | tf_op jit(solution)/shard_map/ppermute | solution.py:41
  115.2 1.1 fusion.24
  116.5 1.0 convolution_convert_fusion.1
  118.3 1.5 collective-permute-start.27
  119.8 1.0 convolution_convert_fusion
  120.8 1.9 collective-permute-start.32
  122.7 7.4 %collective-permute-done.30 = bf16[256,1024]{1,0:T(8,128)(2,1)S(1)} collective-permute-done((bf16[256,1024]{1,0:T(8,128)(2,1)S(1)}, bf16[256,1024]{1,0:T(8,128)(2,1)S(1)}, u32[]{:S(2)}, u32[]{:S(2)}) %collective-permute-start.30) | collective-permute-done | bytes 524320 | tf_op jit(solution)/shard_map/ppermute | solution.py:41
  130.1 1.0 fusion.27
  131.8 3.9 %collective-permute-done.27 = bf16[256,512]{1,0:T(8,128)(2,1)S(1)} collective-permute-done((bf16[256,512]{1,0:T(8,128)(2,1)S(1)}, bf16[256,512]{1,0:T(8,128)(2,1)S(1)}, u32[]{:S(2)}, u32[]{:S(2)}) %collective-permute-start.27) | collective-permute-done | bytes 262176 | tf_op jit(solution)/shard_map/ppermute | solution.py:41
  136.3 3.3 %collective-permute-start.29 = (bf16[256,512]{1,0:T(8,128)(2,1)S(1)}, bf16[256,512]{1,0:T(8,128)(2,1)S(1)}, u32[]{:S(2)}, u32[]{:S(2)}) collective-permute-start(bf16[256,512]{1,0:T(8,128)(2,1)S(1)} %convolution_convert_fusion.4), channel_id=1, source_target_pairs={{0,48},{2,18},{1,49},{3,19},{64,112},{66,82},{65,113},{67,83},{4,5... | collective-permute-start | bytes 786440 | tf_op jit(solution)/shard_map/ppermute | solution.py:41
  139.6 2.4 collective-permute-done.31
  142.0 9.6 %collective-permute-start.28 = (bf16[256,512]{1,0:T(8,128)(2,1)S(1)}, bf16[256,512]{1,0:T(8,128)(2,1)S(1)}, u32[]{:S(2)}, u32[]{:S(2)}) collective-permute-start(bf16[256,512]{1,0:T(8,128)(2,1)S(1)} %fusion.31), channel_id=1, source_target_pairs={{0,16},{2,50},{1,17},{3,51},{64,80},{66,114},{65,81},{67,115},{4,2... | collective-permute-start | bytes 786440 | tf_op jit(solution)/shard_map/ppermute | solution.py:41
  151.6 1.1 fusion.25
  152.7 6.5 %collective-permute-done.28 = bf16[256,512]{1,0:T(8,128)(2,1)S(1)} collective-permute-done((bf16[256,512]{1,0:T(8,128)(2,1)S(1)}, bf16[256,512]{1,0:T(8,128)(2,1)S(1)}, u32[]{:S(2)}, u32[]{:S(2)}) %collective-permute-start.28) | collective-permute-done | bytes 262176 | tf_op jit(solution)/shard_map/ppermute | solution.py:41
  159.1 0.8 fusion.148
  160.1 0.8 fusion.151
  161.0 0.7 collective-permute-done.33
  162.1 1.3 collective-permute-done.18
  163.5 1.6 collective-permute-start.19
  165.0 1.8 collective-permute-start.35
  166.8 6.9 %collective-permute-done.34 = bf16[128,2048]{1,0:T(8,128)(2,1)S(1)} collective-permute-done((bf16[128,2048]{1,0:T(8,128)(2,1)S(1)}, bf16[128,2048]{1,0:T(8,128)(2,1)S(1)}, u32[]{:S(2)}, u32[]{:S(2)}) %collective-permute-start.34) | collective-permute-done | bytes 524320 | tf_op jit(solution)/shard_map/ppermute | solution.py:41
  173.8 3.2 %collective-permute-start.20 = (bf16[128,2048]{1,0:T(8,128)(2,1)S(1)}, bf16[128,2048]{1,0:T(8,128)(2,1)S(1)}, u32[]{:S(2)}, u32[]{:S(2)}) collective-permute-start(bf16[128,2048]{1,0:T(8,128)(2,1)S(1)} %pad_maximum_fusion.7), channel_id=1, source_target_pairs={{0,48},{2,18},{1,49},{3,19},{64,112},{66,82},{65,113},{67,83},{4,5... | collective-permute-start | bytes 1572872 | tf_op jit(solution)/shard_map/ppermute | solution.py:41
  177.0 8.0 %collective-permute-done.19 = bf16[128,2048]{1,0:T(8,128)(2,1)S(1)} collective-permute-done((bf16[128,2048]{1,0:T(8,128)(2,1)S(1)}, bf16[128,2048]{1,0:T(8,128)(2,1)S(1)}, u32[]{:S(2)}, u32[]{:S(2)}) %collective-permute-start.19) | collective-permute-done | bytes 524320 | tf_op jit(solution)/shard_map/ppermute | solution.py:41
  185.0 9.6 %collective-permute-done.36 = bf16[128,2048]{1,0:T(8,128)(2,1)S(1)} collective-permute-done((bf16[128,2048]{1,0:T(8,128)(2,1)S(1)}, bf16[128,2048]{1,0:T(8,128)(2,1)S(1)}, u32[]{:S(2)}, u32[]{:S(2)}) %collective-permute-start.36) | collective-permute-done | bytes 524320 | tf_op jit(solution)/shard_map/ppermute | solution.py:41
  194.6 3.5 %fusion.10 = f32[512,1536]{1,0:T(8,128)S(1)} fusion(bf16[128,2048]{1,0:T(8,128)(2,1)S(1)} %collective-permute-done.36, bf16[128,2048]{1,0:T(8,128)(2,1)S(1)} %collective-permute-done.35, bf16[128,2048]{1,0:T(8,128)(2,1)S(1)} %collective-permute-done.34, bf16[128,1024]{1,0:T(8,128)(2,1)S(1)} %collective-permute-done.33, ...), kind=kOutput, calls=%fused_computation.12 | convolution fusion | flops 3269459968 | bytes 11534336 | tf_op jit(solution)/shard_map/dot_general | solution.py:127
  198.3 2.0 collective-permute-done.21
  200.2 3.5 %fusion = f32[512,1536]{1,0:T(8,128)S(1)} fusion(bf16[128,2048]{1,0:T(8,128)(2,1)S(1)} %collective-permute-done.21, bf16[128,2048]{1,0:T(8,128)(2,1)S(1)} %collective-permute-done.20, bf16[128,2048]{1,0:T(8,128)(2,1)S(1)} %collective-permute-done.19, bf16[128,1024]{1,0:T(8,128)(2,1)S(1)} %collective-permute-done.18, ...), kind=kOutput, calls=%fused_computation.2 | convolution fusion | flops 3269459968 | bytes 11534336 | tf_op jit(solution)/shard_map/dot_general | solution.py:127
  203.8 1.3 collective-permute-start.39
  205.1 12.0 %collective-permute-done.37 = bf16[4,64,1536]{2,1,0:T(8,128)(2,1)S(1)} collective-permute-done((bf16[4,64,1536]{2,1,0:T(8,128)(2,1)S(1)}, bf16[4,64,1536]{2,1,0:T(8,128)(2,1)S(1)}, u32[]{:S(2)}, u32[]{:S(2)}) %collective-permute-start.37) | collective-permute-done | bytes 786464 | tf_op jit(solution)/shard_map/ppermute | solution.py:41
  217.3 4.0 %collective-permute-done.39 = bf16[4,64,1536]{2,1,0:T(8,128)(2,1)S(1)} collective-permute-done((bf16[4,64,1536]{2,1,0:T(8,128)(2,1)S(1)}, bf16[4,64,1536]{2,1,0:T(8,128)(2,1)S(1)}, u32[]{:S(2)}, u32[]{:S(2)}) %collective-permute-start.39) | collective-permute-done | bytes 786464 | tf_op jit(solution)/shard_map/ppermute | solution.py:41
  221.3 9.2 %collective-permute-done.38 = bf16[4,64,1536]{2,1,0:T(8,128)(2,1)S(1)} collective-permute-done((bf16[4,64,1536]{2,1,0:T(8,128)(2,1)S(1)}, bf16[4,64,1536]{2,1,0:T(8,128)(2,1)S(1)}, u32[]{:S(2)}, u32[]{:S(2)}) %collective-permute-start.38) | collective-permute-done | bytes 786464 | tf_op jit(solution)/shard_map/ppermute | solution.py:41
  231.0 9.8 %collective-permute-done.40 = f32[4,64,384]{2,1,0:T(8,128)S(1)} collective-permute-done((f32[4,64,384]{2,1,0:T(8,128)S(1)}, f32[4,64,384]{2,1,0:T(8,128)S(1)}, u32[]{:S(2)}, u32[]{:S(2)}) %collective-permute-start.40) | collective-permute-done | bytes 393248 | tf_op jit(solution)/shard_map/ppermute | solution.py:41
  240.8 1.1 collective-permute-start.41
  241.9 4.0 %collective-permute-start.42 = (f32[4,64,384]{2,1,0:T(8,128)S(1)}, f32[4,64,384]{2,1,0:T(8,128)S(1)}, u32[]{:S(2)}, u32[]{:S(2)}) collective-permute-start(f32[4,64,384]{2,1,0:T(8,128)S(1)} %get-tuple-element.6), channel_id=1, source_target_pairs={{0,65},{2,3},{1,0},{3,66},{64,1},{66,67},{65,64},{67,2},{4,69},{6,... | collective-permute-start | bytes 1179656 | tf_op jit(solution)/shard_map/ppermute | solution.py:41
  254.2 0.7 pad_maximum_fusion.12
  (93 shorter events, 11.0 us)
Async XLA Ops:
  2.8 15.2 %collective-permute-start.1 = (bf16[2,256,384]{2,1,0:T(8,128)(2,1)}, bf16[2,256,384]{2,1,0:T(8,128)(2,1)}, u32[]{:S(2)}, u32[]{:S(2)}) collective-permute-start(bf16[2,256,384]{2,1,0:T(8,128)(2,1)} %pad_maximum_fusion.9), channel_id=1, source_target_pairs={{0,65},{2,3},{1,0},{3,66},{64,1},{66,67},{65,64},{67,2},{4,69},{6,... | collective-permute-start | bytes 1179656 | tf_op jit(solution)/shard_map/ppermute | solution.py:41
  6.8 10.9 %collective-permute-start = (bf16[2,256,384]{2,1,0:T(8,128)(2,1)}, bf16[2,256,384]{2,1,0:T(8,128)(2,1)}, u32[]{:S(2)}, u32[]{:S(2)}) collective-permute-start(bf16[2,256,384]{2,1,0:T(8,128)(2,1)} %pad_maximum_fusion.9), channel_id=1, source_target_pairs={{0,1},{2,67},{1,64},{3,2},{64,65},{66,3},{65,0},{67,66},{4,5},{6,7... | collective-permute-start | bytes 1179656 | tf_op jit(solution)/shard_map/ppermute | solution.py:41
  6.8 5.9 %copy-start = (bf16[384,2048]{1,0:T(8,128)(2,1)S(1)}, bf16[384,2048]{1,0:T(8,128)(2,1)}, u32[]{:S(2)}) copy-start(bf16[384,2048]{1,0:T(8,128)(2,1)} %param.8) | copy-start | bytes 4718596
  6.8 5.9 %copy-start.1 = (bf16[384,2048]{1,0:T(8,128)(2,1)S(1)}, bf16[384,2048]{1,0:T(8,128)(2,1)}, u32[]{:S(2)}) copy-start(bf16[384,2048]{1,0:T(8,128)(2,1)} %param.7) | copy-start | bytes 4718596
  9.5 26.5 %collective-permute-start.6 = (bf16[512,384]{1,0:T(8,128)(2,1)}, bf16[512,384]{1,0:T(8,128)(2,1)}, u32[]{:S(2)}, u32[]{:S(2)}) collective-permute-start(bf16[512,384]{1,0:T(8,128)(2,1)} %get-tuple-element.38), channel_id=1, source_target_pairs={{0,1},{2,67},{1,64},{3,2},{64,65},{66,3},{65,0},{67,66},{4,5},{6,7... | collective-permute-start | bytes 1179656 | tf_op jit(solution)/shard_map/ppermute | solution.py:41
  9.5 26.8 %collective-permute-start.7 = (bf16[512,384]{1,0:T(8,128)(2,1)}, bf16[512,384]{1,0:T(8,128)(2,1)}, u32[]{:S(2)}, u32[]{:S(2)}) collective-permute-start(bf16[512,384]{1,0:T(8,128)(2,1)} %get-tuple-element.40), channel_id=1, source_target_pairs={{0,65},{2,3},{1,0},{3,66},{64,1},{66,67},{65,64},{67,2},{4,69},{6,... | collective-permute-start | bytes 1179656 | tf_op jit(solution)/shard_map/ppermute | solution.py:41
  13.3 31.4 %collective-permute-start.13 = (bf16[384,1024]{1,0:T(8,128)(2,1)S(1)}, bf16[384,1024]{1,0:T(8,128)(2,1)}, u32[]{:S(2)}, u32[]{:S(2)}) collective-permute-start(bf16[384,1024]{1,0:T(8,128)(2,1)S(1)} %pad_maximum_fusion.5), channel_id=1, source_target_pairs={{0,65},{2,3},{1,0},{3,66},{64,1},{66,67},{65,64},{67,2},{4,69},{6,... | collective-permute-start | bytes 2359304 | tf_op jit(solution)/shard_map/ppermute | solution.py:41
  17.8 16.7 %collective-permute-start.2 = (bf16[2,256,384]{2,1,0:T(8,128)(2,1)}, bf16[2,256,384]{2,1,0:T(8,128)(2,1)S(1)}, u32[]{:S(2)}, u32[]{:S(2)}) collective-permute-start(bf16[2,256,384]{2,1,0:T(8,128)(2,1)} %collective-permute-done), channel_id=1, source_target_pairs={{0,1},{2,67},{1,64},{3,2},{64,65},{66,3},{65,0},{67,66},{4,5},{6,7... | collective-permute-start | bytes 1179656 | tf_op jit(solution)/shard_map/ppermute | solution.py:41
  17.9 17.9 %copy-start.2 = (bf16[256,384]{1,0:T(8,128)(2,1)S(1)}, bf16[256,384]{1,0:T(8,128)(2,1)}, u32[]{:S(2)}) copy-start(bf16[256,384]{1,0:T(8,128)(2,1)} %param.5) | copy-start | bytes 589828
  18.0 32.2 %collective-permute-start.12 = (bf16[384,1024]{1,0:T(8,128)(2,1)S(1)}, bf16[384,1024]{1,0:T(8,128)(2,1)S(1)}, u32[]{:S(2)}, u32[]{:S(2)}) collective-permute-start(bf16[384,1024]{1,0:T(8,128)(2,1)S(1)} %pad_maximum_fusion.4), channel_id=1, source_target_pairs={{0,1},{2,67},{1,64},{3,2},{64,65},{66,3},{65,0},{67,66},{4,5},{6,7... | collective-permute-start | bytes 2359304 | tf_op jit(solution)/shard_map/ppermute | solution.py:41
  34.5 37.0 %collective-permute-start.14 = (bf16[384,1024]{1,0:T(8,128)(2,1)S(1)}, bf16[384,1024]{1,0:T(8,128)(2,1)S(1)}, u32[]{:S(2)}, u32[]{:S(2)}) collective-permute-start(bf16[384,1024]{1,0:T(8,128)(2,1)S(1)} %pad_maximum_fusion.6), channel_id=1, source_target_pairs={{0,64},{2,66},{1,65},{3,67},{64,0},{66,2},{65,1},{67,3},{4,68},{6,... | collective-permute-start | bytes 2359304 | tf_op jit(solution)/shard_map/ppermute | solution.py:41
  36.0 8.6 %copy-start.4 = (bf16[512,384]{1,0:T(8,128)(2,1)S(1)}, bf16[512,384]{1,0:T(8,128)(2,1)}, u32[]{:S(2)}) copy-start(bf16[512,384]{1,0:T(8,128)(2,1)} %get-tuple-element.39) | copy-start | bytes 1179652
  36.0 38.9 %collective-permute-start.23 = (bf16[2,256,1536]{2,1,0:T(8,128)(2,1)S(1)}, bf16[2,256,1536]{2,1,0:T(8,128)(2,1)S(1)}, u32[]{:S(2)}, u32[]{:S(2)}) collective-permute-start(bf16[2,256,1536]{2,1,0:T(8,128)(2,1)S(1)} %pad_maximum_fusion.2), channel_id=1, source_target_pairs={{0,4},{2,14},{1,5},{3,15},{64,68},{66,78},{65,69},{67,79},{4,8},{6... | collective-permute-start | bytes 4718600 | tf_op jit(solution)/shard_map/ppermute | solution.py:41
  36.3 39.2 %collective-permute-start.3 = (bf16[2,256,1536]{2,1,0:T(8,128)(2,1)S(1)}, bf16[2,256,1536]{2,1,0:T(8,128)(2,1)S(1)}, u32[]{:S(2)}, u32[]{:S(2)}) collective-permute-start(bf16[2,256,1536]{2,1,0:T(8,128)(2,1)S(1)} %pad_maximum_fusion.2), channel_id=1, source_target_pairs={{0,12},{2,6},{1,13},{3,7},{64,76},{66,70},{65,77},{67,71},{4,0},{6... | collective-permute-start | bytes 4718600 | tf_op jit(solution)/shard_map/ppermute | solution.py:41
  44.6 40.6 %collective-permute-start.8 = (bf16[512,384]{1,0:T(8,128)(2,1)S(1)}, bf16[512,384]{1,0:T(8,128)(2,1)S(1)}, u32[]{:S(2)}, u32[]{:S(2)}) collective-permute-start(bf16[512,384]{1,0:T(8,128)(2,1)S(1)} %copy-done.4), channel_id=1, source_target_pairs={{0,64},{2,66},{1,65},{3,67},{64,0},{66,2},{65,1},{67,3},{4,68},{6,... | collective-permute-start | bytes 1179656 | tf_op jit(solution)/shard_map/ppermute | solution.py:41
  50.3 25.8 %collective-permute-start.5 = (bf16[2,256,1536]{2,1,0:T(8,128)(2,1)S(1)}, bf16[2,256,1536]{2,1,0:T(8,128)(2,1)S(1)}, u32[]{:S(2)}, u32[]{:S(2)}) collective-permute-start(bf16[2,256,1536]{2,1,0:T(8,128)(2,1)S(1)} %pad_maximum_fusion.2), channel_id=1, source_target_pairs={{0,2},{2,0},{1,3},{3,1},{64,66},{66,64},{65,67},{67,65},{4,6},{6,4... | collective-permute-start | bytes 4718600 | tf_op jit(solution)/shard_map/ppermute | solution.py:41
  74.7 110.3 %collective-permute-start.22 = (bf16[1536,1024]{1,0:T(8,128)(2,1)S(1)}, bf16[1536,1024]{1,0:T(8,128)(2,1)S(1)}, u32[]{:S(2)}, u32[]{:S(2)}) collective-permute-start(bf16[1536,1024]{1,0:T(8,128)(2,1)S(1)} %pad_maximum_fusion.1), channel_id=1, source_target_pairs={{0,2},{2,0},{1,3},{3,1},{64,66},{66,64},{65,67},{67,65},{4,6},{6,4... | collective-permute-start | bytes 9437192 | tf_op jit(solution)/shard_map/ppermute | solution.py:41
  74.9 24.5 %collective-permute-start.26 = (bf16[2,256,1536]{2,1,0:T(8,128)(2,1)S(1)}, bf16[2,256,1536]{2,1,0:T(8,128)(2,1)S(1)}, u32[]{:S(2)}, u32[]{:S(2)}) collective-permute-start(bf16[2,256,1536]{2,1,0:T(8,128)(2,1)S(1)} %collective-permute-done.23), channel_id=1, source_target_pairs={{0,2},{2,0},{1,3},{3,1},{64,66},{66,64},{65,67},{67,65},{4,6},{6,4... | collective-permute-start | bytes 4718600 | tf_op jit(solution)/shard_map/ppermute | solution.py:41
  75.5 9.4 %collective-permute-start.4 = (bf16[2,256,1536]{2,1,0:T(8,128)(2,1)S(1)}, bf16[2,256,1536]{2,1,0:T(8,128)(2,1)S(1)}, u32[]{:S(2)}, u32[]{:S(2)}) collective-permute-start(bf16[2,256,1536]{2,1,0:T(8,128)(2,1)S(1)} %collective-permute-done.3), channel_id=1, source_target_pairs={{0,2},{2,0},{1,3},{3,1},{64,66},{66,64},{65,67},{67,65},{4,6},{6,4... | collective-permute-start | bytes 4718600 | tf_op jit(solution)/shard_map/ppermute | solution.py:41
  76.1 20.5 %collective-permute-start.24 = (bf16[2,256,1536]{2,1,0:T(8,128)(2,1)S(1)}, bf16[2,256,1536]{2,1,0:T(8,128)(2,1)S(1)}, u32[]{:S(2)}, u32[]{:S(2)}) collective-permute-start(bf16[2,256,1536]{2,1,0:T(8,128)(2,1)S(1)} %collective-permute-done.23), channel_id=1, source_target_pairs={{0,4},{2,14},{1,5},{3,15},{64,68},{66,78},{65,69},{67,79},{4,8},{6... | collective-permute-start | bytes 4718600 | tf_op jit(solution)/shard_map/ppermute | solution.py:41
  85.1 1.0 copy-start.3
  86.7 15.4 %collective-permute-start.9 = (bf16[256,512]{1,0:T(8,128)(2,1)S(1)}, bf16[256,512]{1,0:T(8,128)(2,1)S(1)}, u32[]{:S(2)}, u32[]{:S(2)}) collective-permute-start(bf16[256,512]{1,0:T(8,128)(2,1)S(1)} %convolution_convert_fusion.7), channel_id=1, source_target_pairs={{0,16},{2,50},{1,17},{3,51},{64,80},{66,114},{65,81},{67,115},{4,2... | collective-permute-start | bytes 786440 | tf_op jit(solution)/shard_map/ppermute | solution.py:41
  89.4 10.7 %collective-permute-start.15 = (bf16[256,1024]{1,0:T(8,128)(2,1)S(1)}, bf16[256,1024]{1,0:T(8,128)(2,1)S(1)}, u32[]{:S(2)}, u32[]{:S(2)}) collective-permute-start(bf16[256,1024]{1,0:T(8,128)(2,1)S(1)} %convolution_convert_fusion.3), channel_id=1, source_target_pairs={{0,16},{2,50},{1,17},{3,51},{64,80},{66,114},{65,81},{67,115},{4,2... | collective-permute-start | bytes 1572872 | tf_op jit(solution)/shard_map/ppermute | solution.py:41
  96.6 12.6 %collective-permute-start.17 = (bf16[256,1024]{1,0:T(8,128)(2,1)S(1)}, bf16[256,1024]{1,0:T(8,128)(2,1)S(1)}, u32[]{:S(2)}, u32[]{:S(2)}) collective-permute-start(bf16[256,1024]{1,0:T(8,128)(2,1)S(1)} %convolution_convert_fusion.2), channel_id=1, source_target_pairs={{0,48},{2,18},{1,49},{3,19},{64,112},{66,82},{65,113},{67,83},{4,5... | collective-permute-start | bytes 1572872 | tf_op jit(solution)/shard_map/ppermute | solution.py:41
  99.4 16.8 %collective-permute-start.25 = (bf16[2,256,1536]{2,1,0:T(8,128)(2,1)S(1)}, bf16[2,256,1536]{2,1,0:T(8,128)(2,1)S(1)}, u32[]{:S(2)}, u32[]{:S(2)}) collective-permute-start(bf16[2,256,1536]{2,1,0:T(8,128)(2,1)S(1)} %collective-permute-done.24), channel_id=1, source_target_pairs={{0,2},{2,0},{1,3},{3,1},{64,66},{66,64},{65,67},{67,65},{4,6},{6,4... | collective-permute-start | bytes 4718600 | tf_op jit(solution)/shard_map/ppermute | solution.py:41
  101.1 14.1 %collective-permute-start.16 = (bf16[256,1024]{1,0:T(8,128)(2,1)S(1)}, bf16[256,1024]{1,0:T(8,128)(2,1)S(1)}, u32[]{:S(2)}, u32[]{:S(2)}) collective-permute-start(bf16[256,1024]{1,0:T(8,128)(2,1)S(1)} %fusion.26), channel_id=1, source_target_pairs={{0,16},{2,50},{1,17},{3,51},{64,80},{66,114},{65,81},{67,115},{4,2... | collective-permute-start | bytes 1572872 | tf_op jit(solution)/shard_map/ppermute | solution.py:41
  102.1 58.1 %collective-permute-start.11 = (bf16[256,512]{1,0:T(8,128)(2,1)S(1)}, bf16[256,512]{1,0:T(8,128)(2,1)S(1)}, u32[]{:S(2)}, u32[]{:S(2)}) collective-permute-start(bf16[256,512]{1,0:T(8,128)(2,1)S(1)} %convolution_convert_fusion.6), channel_id=1, source_target_pairs={{0,48},{2,18},{1,49},{3,19},{64,112},{66,82},{65,113},{67,83},{4,5... | collective-permute-start | bytes 786440 | tf_op jit(solution)/shard_map/ppermute | solution.py:41
  117.5 12.6 %collective-permute-start.30 = (bf16[256,1024]{1,0:T(8,128)(2,1)S(1)}, bf16[256,1024]{1,0:T(8,128)(2,1)S(1)}, u32[]{:S(2)}, u32[]{:S(2)}) collective-permute-start(bf16[256,1024]{1,0:T(8,128)(2,1)S(1)} %convolution_convert_fusion.1), channel_id=1, source_target_pairs={{0,16},{2,50},{1,17},{3,51},{64,80},{66,114},{65,81},{67,115},{4,2... | collective-permute-start | bytes 1572872 | tf_op jit(solution)/shard_map/ppermute | solution.py:41
  118.3 17.4 %collective-permute-start.27 = (bf16[256,512]{1,0:T(8,128)(2,1)S(1)}, bf16[256,512]{1,0:T(8,128)(2,1)S(1)}, u32[]{:S(2)}, u32[]{:S(2)}) collective-permute-start(bf16[256,512]{1,0:T(8,128)(2,1)S(1)} %convolution_convert_fusion.5), channel_id=1, source_target_pairs={{0,16},{2,50},{1,17},{3,51},{64,80},{66,114},{65,81},{67,115},{4,2... | collective-permute-start | bytes 786440 | tf_op jit(solution)/shard_map/ppermute | solution.py:41
  120.8 15.5 %collective-permute-start.32 = (bf16[256,1024]{1,0:T(8,128)(2,1)S(1)}, bf16[256,1024]{1,0:T(8,128)(2,1)S(1)}, u32[]{:S(2)}, u32[]{:S(2)}) collective-permute-start(bf16[256,1024]{1,0:T(8,128)(2,1)S(1)} %convolution_convert_fusion), channel_id=1, source_target_pairs={{0,48},{2,18},{1,49},{3,19},{64,112},{66,82},{65,113},{67,83},{4,5... | collective-permute-start | bytes 1572872 | tf_op jit(solution)/shard_map/ppermute | solution.py:41
  131.1 10.9 %collective-permute-start.31 = (bf16[256,1024]{1,0:T(8,128)(2,1)S(1)}, bf16[256,1024]{1,0:T(8,128)(2,1)S(1)}, u32[]{:S(2)}, u32[]{:S(2)}) collective-permute-start(bf16[256,1024]{1,0:T(8,128)(2,1)S(1)} %fusion.27), channel_id=1, source_target_pairs={{0,16},{2,50},{1,17},{3,51},{64,80},{66,114},{65,81},{67,115},{4,2... | collective-permute-start | bytes 1572872 | tf_op jit(solution)/shard_map/ppermute | solution.py:41
  135.7 24.4 %collective-permute-start.10 = (bf16[256,512]{1,0:T(8,128)(2,1)S(1)}, bf16[256,512]{1,0:T(8,128)(2,1)S(1)}, u32[]{:S(2)}, u32[]{:S(2)}) collective-permute-start(bf16[256,512]{1,0:T(8,128)(2,1)S(1)} %fusion.30), channel_id=1, source_target_pairs={{0,16},{2,50},{1,17},{3,51},{64,80},{66,114},{65,81},{67,115},{4,2... | collective-permute-start | bytes 786440 | tf_op jit(solution)/shard_map/ppermute | solution.py:41
  136.3 16.4 %collective-permute-start.29 = (bf16[256,512]{1,0:T(8,128)(2,1)S(1)}, bf16[256,512]{1,0:T(8,128)(2,1)S(1)}, u32[]{:S(2)}, u32[]{:S(2)}) collective-permute-start(bf16[256,512]{1,0:T(8,128)(2,1)S(1)} %convolution_convert_fusion.4), channel_id=1, source_target_pairs={{0,48},{2,18},{1,49},{3,19},{64,112},{66,82},{65,113},{67,83},{4,5... | collective-permute-start | bytes 786440 | tf_op jit(solution)/shard_map/ppermute | solution.py:41
  142.0 17.2 %collective-permute-start.28 = (bf16[256,512]{1,0:T(8,128)(2,1)S(1)}, bf16[256,512]{1,0:T(8,128)(2,1)S(1)}, u32[]{:S(2)}, u32[]{:S(2)}) collective-permute-start(bf16[256,512]{1,0:T(8,128)(2,1)S(1)} %fusion.31), channel_id=1, source_target_pairs={{0,16},{2,50},{1,17},{3,51},{64,80},{66,114},{65,81},{67,115},{4,2... | collective-permute-start | bytes 786440 | tf_op jit(solution)/shard_map/ppermute | solution.py:41
  160.0 1.6 collective-permute-start.33
  161.7 12.1 %collective-permute-start.34 = (bf16[128,2048]{1,0:T(8,128)(2,1)S(1)}, bf16[128,2048]{1,0:T(8,128)(2,1)S(1)}, u32[]{:S(2)}, u32[]{:S(2)}) collective-permute-start(bf16[128,2048]{1,0:T(8,128)(2,1)S(1)} %pad_maximum_fusion.8), channel_id=1, source_target_pairs={{0,16},{2,50},{1,17},{3,51},{64,80},{66,114},{65,81},{67,115},{4,2... | collective-permute-start | bytes 1572872 | tf_op jit(solution)/shard_map/ppermute | solution.py:41
  161.8 1.6 collective-permute-start.18
  163.5 21.5 %collective-permute-start.19 = (bf16[128,2048]{1,0:T(8,128)(2,1)S(1)}, bf16[128,2048]{1,0:T(8,128)(2,1)S(1)}, u32[]{:S(2)}, u32[]{:S(2)}) collective-permute-start(bf16[128,2048]{1,0:T(8,128)(2,1)S(1)} %pad_maximum_fusion.7), channel_id=1, source_target_pairs={{0,16},{2,50},{1,17},{3,51},{64,80},{66,114},{65,81},{67,115},{4,2... | collective-permute-start | bytes 1572872 | tf_op jit(solution)/shard_map/ppermute | solution.py:41
  165.0 20.0 %collective-permute-start.35 = (bf16[128,2048]{1,0:T(8,128)(2,1)S(1)}, bf16[128,2048]{1,0:T(8,128)(2,1)S(1)}, u32[]{:S(2)}, u32[]{:S(2)}) collective-permute-start(bf16[128,2048]{1,0:T(8,128)(2,1)S(1)} %pad_maximum_fusion.8), channel_id=1, source_target_pairs={{0,48},{2,18},{1,49},{3,19},{64,112},{66,82},{65,113},{67,83},{4,5... | collective-permute-start | bytes 1572872 | tf_op jit(solution)/shard_map/ppermute | solution.py:41
  173.8 20.8 %collective-permute-start.36 = (bf16[128,2048]{1,0:T(8,128)(2,1)S(1)}, bf16[128,2048]{1,0:T(8,128)(2,1)S(1)}, u32[]{:S(2)}, u32[]{:S(2)}) collective-permute-start(bf16[128,2048]{1,0:T(8,128)(2,1)S(1)} %collective-permute-done.34), channel_id=1, source_target_pairs={{0,16},{2,50},{1,17},{3,51},{64,80},{66,114},{65,81},{67,115},{4,2... | collective-permute-start | bytes 1572872 | tf_op jit(solution)/shard_map/ppermute | solution.py:41
  173.8 24.5 %collective-permute-start.20 = (bf16[128,2048]{1,0:T(8,128)(2,1)S(1)}, bf16[128,2048]{1,0:T(8,128)(2,1)S(1)}, u32[]{:S(2)}, u32[]{:S(2)}) collective-permute-start(bf16[128,2048]{1,0:T(8,128)(2,1)S(1)} %pad_maximum_fusion.7), channel_id=1, source_target_pairs={{0,48},{2,18},{1,49},{3,19},{64,112},{66,82},{65,113},{67,83},{4,5... | collective-permute-start | bytes 1572872 | tf_op jit(solution)/shard_map/ppermute | solution.py:41
  185.0 15.2 %collective-permute-start.21 = (bf16[128,2048]{1,0:T(8,128)(2,1)S(1)}, bf16[128,2048]{1,0:T(8,128)(2,1)S(1)}, u32[]{:S(2)}, u32[]{:S(2)}) collective-permute-start(bf16[128,2048]{1,0:T(8,128)(2,1)S(1)} %collective-permute-done.19), channel_id=1, source_target_pairs={{0,16},{2,50},{1,17},{3,51},{64,80},{66,114},{65,81},{67,115},{4,2... | collective-permute-start | bytes 1572872 | tf_op jit(solution)/shard_map/ppermute | solution.py:41
  198.2 18.9 %collective-permute-start.37 = (bf16[4,64,1536]{2,1,0:T(8,128)(2,1)S(1)}, bf16[4,64,1536]{2,1,0:T(8,128)(2,1)S(1)}, u32[]{:S(2)}, u32[]{:S(2)}) collective-permute-start(bf16[4,64,1536]{2,1,0:T(8,128)(2,1)S(1)} %fusion.33), channel_id=1, source_target_pairs={{0,12},{2,6},{1,13},{3,7},{64,76},{66,70},{65,77},{67,71},{4,0},{6... | collective-permute-start | bytes 2359304 | tf_op jit(solution)/shard_map/ppermute | solution.py:41
  203.8 17.5 %collective-permute-start.39 = (bf16[4,64,1536]{2,1,0:T(8,128)(2,1)S(1)}, bf16[4,64,1536]{2,1,0:T(8,128)(2,1)S(1)}, u32[]{:S(2)}, u32[]{:S(2)}) collective-permute-start(bf16[4,64,1536]{2,1,0:T(8,128)(2,1)S(1)} %fusion.32), channel_id=1, source_target_pairs={{0,4},{2,14},{1,5},{3,15},{64,68},{66,78},{65,69},{67,79},{4,8},{6... | collective-permute-start | bytes 2359304 | tf_op jit(solution)/shard_map/ppermute | solution.py:41
  217.3 13.3 %collective-permute-start.38 = (bf16[4,64,1536]{2,1,0:T(8,128)(2,1)S(1)}, bf16[4,64,1536]{2,1,0:T(8,128)(2,1)S(1)}, u32[]{:S(2)}, u32[]{:S(2)}) collective-permute-start(bf16[4,64,1536]{2,1,0:T(8,128)(2,1)S(1)} %fusion.21), channel_id=1, source_target_pairs={{0,12},{2,6},{1,13},{3,7},{64,76},{66,70},{65,77},{67,71},{4,0},{6... | collective-permute-start | bytes 2359304 | tf_op jit(solution)/shard_map/ppermute | solution.py:41
  230.9 9.9 %collective-permute-start.40 = (f32[4,64,384]{2,1,0:T(8,128)S(1)}, f32[4,64,384]{2,1,0:T(8,128)S(1)}, u32[]{:S(2)}, u32[]{:S(2)}) collective-permute-start(f32[4,64,384]{2,1,0:T(8,128)S(1)} %slice.209), channel_id=1, source_target_pairs={{0,1},{2,67},{1,64},{3,2},{64,65},{66,3},{65,0},{67,66},{4,5},{6,7... | collective-permute-start | bytes 1179656 | tf_op jit(solution)/shard_map/ppermute | solution.py:41
  240.8 13.3 %collective-permute-start.41 = (f32[4,64,384]{2,1,0:T(8,128)S(1)}, f32[4,64,384]{2,1,0:T(8,128)S(1)}, u32[]{:S(2)}, u32[]{:S(2)}) collective-permute-start(f32[4,64,384]{2,1,0:T(8,128)S(1)} %get-tuple-element.5), channel_id=1, source_target_pairs={{0,1},{2,67},{1,64},{3,2},{64,65},{66,3},{65,0},{67,66},{4,5},{6,7... | collective-permute-start | bytes 1179656 | tf_op jit(solution)/shard_map/ppermute | solution.py:41
  241.9 12.2 %collective-permute-start.42 = (f32[4,64,384]{2,1,0:T(8,128)S(1)}, f32[4,64,384]{2,1,0:T(8,128)S(1)}, u32[]{:S(2)}, u32[]{:S(2)}) collective-permute-start(f32[4,64,384]{2,1,0:T(8,128)S(1)} %get-tuple-element.6), channel_id=1, source_target_pairs={{0,65},{2,3},{1,0},{3,66},{64,1},{66,67},{65,64},{67,2},{4,69},{6,... | collective-permute-start | bytes 1179656 | tf_op jit(solution)/shard_map/ppermute | solution.py:41

commit v2 on v1

v2 whole, which is shorter than its diff:
```python
import jax
import jax.numpy as jnp
from jax import lax
from jax.experimental import pallas as pl
from jax.experimental.pallas import tpu as pltpu
from jax.sharding import PartitionSpec as P

AXES = ("row", "col", "rep")
SIDE = 4
CHUNKS = ((3, 1), (2, 0))


def place(x, y, z, c):
    return (((z // 2) * SIDE + x) * 2 * SIDE + y * 2 + c) * 2 + z % 2


def pairs(move):
    found = []
    for x in range(SIDE):
        for y in range(SIDE):
            for z in range(SIDE):
                for c in range(2):
                    nx, ny, nz, nc = move(x, y, z, c)
                    found.append((place(x, y, z, c), place(nx % SIDE, ny % SIDE, nz % SIDE, nc)))
    return found


STEPS = (1, -1, 2)
SUM = [pairs(lambda x, y, z, c, n=n: (x + n * (c == 0), y, z + n * (c == 1), c)) for n in STEPS]
SWAP = [pairs(lambda x, y, z, c, n=n: (x + n * (c == 1), y, z + n * (c == 0), c)) for n in STEPS]
AHEAD = pairs(lambda x, y, z, c: (x, y + 1 - 2 * c, z, c))
BEHIND = pairs(lambda x, y, z, c: (x, y - 1 + 2 * c, z, c))
CORES = pairs(lambda x, y, z, c: (x, y, z, 1 - c))


def send(value, route):
    return lax.ppermute(value, AXES, route)


def spread(values, routes):
    return [send(v, route) for v, route in zip(values, routes)]


def after(value, *earlier):
    return lax.optimization_barrier((value, *earlier))[0]


def side_by_side(*refs):
    *ins, out = refs
    width = ins[0].shape[1]
    for k, v in enumerate(ins):
        out[:, k * width : (k + 1) * width] = v[...]


def one_above_other(*refs):
    *ins, out = refs
    for k, v in enumerate(ins):
        out[k] = v[...]


def moved(body, out_shape, grid, in_specs, out_spec, arrays, where=None):
    kernel = body if where is None else (lambda where_ref, *refs: body(*refs))
    size = sum(2 * v.size for v in arrays) + 2 * out_shape.size
    return pl.pallas_call(
        kernel,
        out_shape=out_shape,
        grid_spec=pltpu.PrefetchScalarGridSpec(
            num_scalar_prefetch=0 if where is None else 1,
            grid=grid,
            in_specs=in_specs,
            out_specs=out_spec,
        ),
        compiler_params=pltpu.CompilerParams(vmem_limit_bytes=32 * 2**20),
        cost_estimate=pl.CostEstimate(flops=0, bytes_accessed=size, transcendentals=0),
    )(*(() if where is None else (where.reshape(1),)), *arrays)


ROWS = 128


def quarter(arrays, axis, where):
    rows, cols = arrays[0].shape
    count = len(arrays)
    kind = arrays[0].dtype
    if axis == 1:
        size = cols // SIDE
        return moved(
            side_by_side,
            jax.ShapeDtypeStruct((rows, size * count), kind),
            (rows // ROWS,),
            [pl.BlockSpec((ROWS, size), lambda r, at: (r, at[0]))] * count,
            pl.BlockSpec((ROWS, size * count), lambda r, at: (r, 0)),
            arrays,
            where,
        )
    size = rows // SIDE
    blocks = size // ROWS
    return moved(
        one_above_other,
        jax.ShapeDtypeStruct((count, size, cols), kind),
        (blocks,),
        [pl.BlockSpec((ROWS, cols), lambda r, at: (at[0] * blocks + r, 0))] * count,
        pl.BlockSpec((count, ROWS, cols), lambda r, at: (0, r, 0)),
        arrays,
        where,
    ).reshape(size * count, cols)


def joined(arrays, axis):
    rows, cols = arrays[0].shape
    count = len(arrays)
    kind = arrays[0].dtype
    if axis == 1:
        return moved(
            side_by_side,
            jax.ShapeDtypeStruct((rows, cols * count), kind),
            (rows // ROWS,),
            [pl.BlockSpec((ROWS, cols), lambda r: (r, 0))] * count,
            pl.BlockSpec((ROWS, cols * count), lambda r: (r, 0)),
            arrays,
        )
    return moved(
        one_above_other,
        jax.ShapeDtypeStruct((count, rows, cols), kind),
        (rows // ROWS,),
        [pl.BlockSpec((ROWS, cols), lambda r: (r, 0))] * count,
        pl.BlockSpec((count, ROWS, cols), lambda r: (0, r, 0)),
        arrays,
    ).reshape(rows * count, cols)


def shards(latents, probe, w_gate, w_up, w_down):
    f32, bf16 = jnp.float32, jnp.bfloat16
    row, col = lax.axis_index("row"), lax.axis_index("col")
    x, z = row % SIDE, (row // SIDE) * 2 + lax.axis_index("rep")
    even = col % 2 == 0
    a, b = jnp.where(even, x, z), jnp.where(even, z, x)
    tokens, features = latents.shape
    part = tokens // SIDE

    bits = lax.dynamic_slice_in_dim(probe, col * tokens, tokens, axis=0)
    rows = jnp.stack((latents, (2 * bits - 1).astype(bf16)))
    first = spread([rows] * 3, SWAP)
    others = [send(w, CORES) for w in (w_gate, w_up)]
    others.append(send(after(w_down, *first), CORES))
    rows = jnp.concatenate((rows, *first), axis=2)
    near = send(rows, AHEAD)
    far = send(near, AHEAD)
    slots = [rows, near, send(after(rows, far), BEHIND), far]

    pieces = [quarter((w_gate, others[0], w_up, others[1]), 1, (b + n) % SIDE) for n in (0, *STEPS)]
    gate_up = joined([pieces[0], *spread(pieces[1:], SWAP)], 0)
    pieces = [quarter((w_down, others[2]), 0, (b + n) % SIDE) for n in (0, *STEPS)]
    down = joined([pieces[0], *spread([after(v, far) for v in pieces[1:]], SWAP)], 1)
    width = down.shape[0]

    def summed(terms):
        terms = [v.reshape(SIDE, part, -1) for v in terms]

        def term(step):
            blocks = [lax.dynamic_index_in_dim(v, (a + step) % SIDE, 0, keepdims=False) for v in terms]
            return jnp.concatenate(blocks, axis=0)

        got = spread([term(step).astype(bf16) for step in STEPS], SUM)
        return term(0) + got[0] + got[1] + got[2]

    totals = {}
    for chunk in CHUNKS:
        gate_up_sum = summed([jnp.dot(slots[k][0], gate_up, preferred_element_type=f32) for k in chunk])
        back = summed(
            [
                lax.dot_general(slots[k][1], down, (((1,), (1,)), ((), ())), preferred_element_type=f32)
                for k in chunk
            ]
        )
        gate, up = gate_up_sum[:, :width], gate_up_sum[:, width:]
        sigma = jax.nn.sigmoid(gate)
        slopes = jnp.concatenate(
            (
                (back * up * sigma * (1.0 + gate * (1.0 - sigma))).astype(bf16),
                (back * gate * sigma).astype(bf16),
            ),
            axis=1,
        )
        slopes = jnp.concatenate((slopes, *spread([slopes] * 3, SUM)), axis=0)
        out = lax.dot_general(slopes, gate_up, (((1,), (1,)), ((), ())), preferred_element_type=f32)
        out = out.reshape(SIDE, len(chunk), part, -1)
        for n, slot in enumerate(chunk):
            totals[slot] = out[:, n]

    relay = send(totals[3].astype(bf16), BEHIND)
    near = send((totals[1] + relay).astype(bf16), BEHIND)
    total = totals[0] + near + send(totals[2].astype(bf16), AHEAD)
    own, below, above, far = (total[:, :, n * features : (n + 1) * features] for n in range(SIDE))
    total = own
    for v in spread((above, below, far), SWAP):
        total = total + v
    total = total.astype(bf16)

    source = jnp.array([0, 2, 3, 1], jnp.int32)
    return jnp.concatenate(
        [lax.dynamic_index_in_dim(total, source[(j - a) % SIDE], 0, keepdims=False) for j in range(SIDE)],
        axis=0,
    )


def solution(mesh):
    in_specs = (
        P("col", ("row", "rep")),
        P(None, ("row", "rep")),
        P(("row", "rep"), "col"),
        P(("row", "rep"), "col"),
        P("col", ("row", "rep")),
    )
    out_specs = P("col", ("row", "rep"))
    return jax.shard_map(shards, mesh=mesh, in_specs=in_specs, out_specs=out_specs, check_vma=False)
```

time: 259 us -> 215 us (0.83)
  waiting for transfers between devices: 133 us -> 101 us
  starting transfers between devices: 75 us -> 48.7 us
  Pallas kernels: 0 us -> 16.8 us
    ppermute x43 -> x39, waiting for transfers between devices: 133 us -> 101 us  [send(): return lax.ppermute(value, AXES, route)]
    ppermute x43 -> x39, starting transfers between devices: 75 us -> 48.7 us  [send(): return lax.ppermute(value, AXES, route)]
    pallas_call x0 -> x10, Pallas kernels: none -> 16.8 us  [moved(): pl.pallas_call(kernel, out_shape=out_shape, grid_spec=pltpu.PrefetchScala...]
    dynamic_slice x11 -> x1, local copies, waits for them, and re-layouts: 4.7 us -> 0.65 us  [shards(): source[(j - a) % SIDE]]
    slice x8 -> x4, local copies, waits for them, and re-layouts: 0.82 us -> 4.52 us  [shards(): slots[k][1]]
    select_n x3 -> x0, other arithmetic: 3.62 us -> none  [ordered(): jnp.where(even, near, next_)]
    concatenate x8 -> x16, other arithmetic: 4.29 us -> 7.06 us  [the longest x2 3.78 us: shards(): slopes = jnp.concatenate((slopes, *spread([slopes] * 3, SUM)), axis=0)]
    dot_general x18 -> x10, matrix products: 20.3 us -> 18.1 us  [the longest x4 7.14 us: shards(): jnp.dot(slots[k][0], gate_up, preferred_element_type=f32)]
  transfers between devices with their start and end apart: 43 -> 39, of which waited for: 23 -> 24; matrix products, arithmetic and copies ran while one was open for 13% -> 15% of each run, Pallas kernels for 0% -> 8%
where the time goes in v2:
time: 215 us; the launch traced here: 212 us
  waiting for transfers between devices  101 us (47%)
  starting transfers between devices  48.7 us (23%)
  matrix products  18.1 us (8%)
  Pallas kernels  16.8 us (8%)
  other arithmetic  11.2 us (5%)
  local copies, waits for them, and re-layouts  8.67 us (4%)
  between operations  8.01 us (4%)
    ppermute x39, waiting for transfers between devices, send(): return lax.ppermute(value, AXES, route)  101 us
    ppermute x39, starting transfers between devices, send(): return lax.ppermute(value, AXES, route)  48.7 us
    pallas_call x10, Pallas kernels, moved(): pl.pallas_call(kernel, out_shape=out_shape, grid_spec=pltpu.PrefetchScala...  16.8 us
    dot_general x4, matrix products, shards(): jnp.dot(slots[k][0], gate_up, preferred_element_type=f32)  7.14 us
    dot_general x2, matrix products, shards(): lax.dot_general(slopes, gate_up, (((1,), (1,)), ((), ())), preferred_elem...  6.94 us
    slice x4, local copies, waits for them, and re-layouts, shards(): slots[k][1]  4.52 us
  transfers between devices with their start and end apart: 39, of which 24 were waited for; matrix products, arithmetic and copies ran while one was open for 15% of the time, Pallas kernels for 8%

profile of v2, /device:TPU:24, one launch (start us, length us, event | category | flops | bytes accessed | tf_op | source)
XLA Modules:
  0.0 212.0 jit_solution(1351636245617689226)
XLA Ops:
  0.0 1.0 fusion.45
  1.1 1.1 pad_maximum_fusion.11
  2.2 4.0 %collective-permute-start.2 = (bf16[2,256,384]{2,1,0:T(8,128)(2,1)S(1)}, bf16[2,256,384]{2,1,0:T(8,128)(2,1)S(1)}, u32[]{:S(2)}, u32[]{:S(2)}) collective-permute-start(bf16[2,256,384]{2,1,0:T(8,128)(2,1)S(1)} %pad_maximum_fusion.11), channel_id=1, source_target_pairs={{0,64},{2,34},{1,65},{3,35},{64,0},{66,98},{65,1},{67,99},{4,68},{... | collective-permute-start | bytes 1179656 | tf_op jit(solution)/shard_map/ppermute | solution.py:37
  6.9 1.3 collective-permute-start
  8.7 3.2 %collective-permute-done.2 = bf16[2,256,384]{2,1,0:T(8,128)(2,1)S(1)} collective-permute-done((bf16[2,256,384]{2,1,0:T(8,128)(2,1)S(1)}, bf16[2,256,384]{2,1,0:T(8,128)(2,1)S(1)}, u32[]{:S(2)}, u32[]{:S(2)}) %collective-permute-start.2) | collective-permute-done | bytes 393248 | tf_op jit(solution)/shard_map/ppermute | solution.py:37
  11.9 5.2 %collective-permute-done.1 = bf16[2,256,384]{2,1,0:T(8,128)(2,1)S(1)} collective-permute-done((bf16[2,256,384]{2,1,0:T(8,128)(2,1)S(1)}, bf16[2,256,384]{2,1,0:T(8,128)(2,1)S(1)}, u32[]{:S(2)}, u32[]{:S(2)}) %collective-permute-start.1) | collective-permute-done | bytes 393248 | tf_op jit(solution)/shard_map/ppermute | solution.py:37
  17.2 2.2 %pad_maximum_fusion.2 = bf16[2,256,1536]{2,1,0:T(8,128)(2,1)} fusion(bf16[2,256,384]{2,1,0:T(8,128)(2,1)S(1)} %collective-permute-done.2, bf16[2,256,384]{2,1,0:T(8,128)(2,1)S(1)} %collective-permute-done.1, bf16[2,256,384]{2,1,0:T(8,128)(2,1)S(1)} %collective-permute-done, bf16[1,256,384]{2,1,0:T(8,128)(2,1)S(1)} %fusion.45, bf16[1,256,384]{2,1,0:T(8,128)(2,1)} %bitcast.159), kind=kLoop, calls=%fused_computation.20 | loop fusion | flops 7864320 | bytes 3145728 | tf_op jit(solution)/shard_map/concatenate | solution.py:146
  19.7 3.3 %shard_map.70 = bf16[384,2048]{1,0:T(8,128)(2,1)} custom-call(s32[1]{0:T(128)} %bitcast.5.where_ref, bf16[384,2048]{1,0:T(8,128)(2,1)S(1)} %copy-done.1, bf16[384,2048]{1,0:T(8,128)(2,1)} %collective-permute-done.13.refs_1_, bf16[384,2048]{1,0:T(8,128)(2,1)S(1)} %copy-done.2, bf16[384,2048]{1,0:T(8,128)(2,1)} %collective-permute-done.14.refs_3_), custom_call_target="tpu_custom_call" | custom-call | bytes 7864320 | tf_op jit(solution)/shard_map/pallas_call | solution.py:64
  23.0 1.0 collective-permute-start.15
  24.0 3.3 %shard_map.71 = bf16[384,2048]{1,0:T(8,128)(2,1)} custom-call(s32[1]{0:T(128)} %bitcast.7.where_ref, bf16[384,2048]{1,0:T(8,128)(2,1)S(1)} %copy-done.1, bf16[384,2048]{1,0:T(8,128)(2,1)} %collective-permute-done.13.refs_1_, bf16[384,2048]{1,0:T(8,128)(2,1)S(1)} %copy-done.2, bf16[384,2048]{1,0:T(8,128)(2,1)} %collective-permute-done.14.refs_3_), custom_call_target="tpu_custom_call" | custom-call | bytes 7864320 | tf_op jit(solution)/shard_map/pallas_call | solution.py:64
  27.3 2.2 %collective-permute-start.16 = (bf16[384,2048]{1,0:T(8,128)(2,1)}, bf16[384,2048]{1,0:T(8,128)(2,1)}, u32[]{:S(2)}, u32[]{:S(2)}) collective-permute-start(bf16[384,2048]{1,0:T(8,128)(2,1)} %shard_map.71), channel_id=1, source_target_pairs={{0,65},{2,50},{1,0},{3,51},{64,1},{66,114},{65,64},{67,115},{4,69}... | collective-permute-start | bytes 4718600 | tf_op jit(solution)/shard_map/ppermute | solution.py:37
  29.5 3.4 %shard_map.72 = bf16[384,2048]{1,0:T(8,128)(2,1)} custom-call(s32[1]{0:T(128)} %bitcast.9.where_ref, bf16[384,2048]{1,0:T(8,128)(2,1)S(1)} %copy-done.1, bf16[384,2048]{1,0:T(8,128)(2,1)} %collective-permute-done.13.refs_1_, bf16[384,2048]{1,0:T(8,128)(2,1)S(1)} %copy-done.3, bf16[384,2048]{1,0:T(8,128)(2,1)} %collective-permute-done.14.refs_3_), custom_call_target="tpu_custom_call" | custom-call | bytes 7864320 | tf_op jit(solution)/shard_map/pallas_call | solution.py:64
  32.9 1.3 collective-permute-start.17
  34.2 6.0 %collective-permute-done.3 = bf16[2,256,1536]{2,1,0:T(8,128)(2,1)} collective-permute-done((bf16[2,256,1536]{2,1,0:T(8,128)(2,1)}, bf16[2,256,1536]{2,1,0:T(8,128)(2,1)}, u32[]{:S(2)}, u32[]{:S(2)}) %collective-permute-start.3) | collective-permute-done | bytes 1572896 | tf_op jit(solution)/shard_map/ppermute | solution.py:37
  40.2 1.4 collective-permute-start.4
  41.6 1.4 copy-done.4
  43.0 2.1 shard_map.69.refs_0_
  45.1 1.5 fusion.60
  46.6 18.1 %collective-permute-done.16.refs_2_ = bf16[384,2048]{1,0:T(8,128)(2,1)} collective-permute-done((bf16[384,2048]{1,0:T(8,128)(2,1)}, bf16[384,2048]{1,0:T(8,128)(2,1)}, u32[]{:S(2)}, u32[]{:S(2)}) %collective-permute-start.16) | collective-permute-done | bytes 1572896 | tf_op jit(solution)/shard_map/ppermute | solution.py:37
  64.7 3.3 %shard_map.73 = bf16[4,384,2048]{2,1,0:T(8,128)(2,1)S(1)} custom-call(bf16[384,2048]{1,0:T(8,128)(2,1)S(1)} %shard_map.69.refs_0_, bf16[384,2048]{1,0:T(8,128)(2,1)} %collective-permute-done.15.refs_1_, bf16[384,2048]{1,0:T(8,128)(2,1)} %collective-permute-done.16.refs_2_, bf16[384,2048]{1,0:T(8,128)(2,1)} %collective-permute-done.17.refs_3_), custom_call_target="tpu_custom_call" | custom-call | bytes 12582912 | tf_op jit(solution)/shard_map/pallas_call | solution.py:64
  68.0 1.8 fusion.68
  69.8 1.5 fusion.59
  71.3 1.8 fusion.67
  73.4 2.8 %collective-permute-start.28 = (bf16[128,2048]{1,0:T(8,128)(2,1)S(1)}, bf16[128,2048]{1,0:T(8,128)(2,1)S(1)}, u32[]{:S(2)}, u32[]{:S(2)}) collective-permute-start(bf16[128,2048]{1,0:T(8,128)(2,1)S(1)} %pad_maximum_fusion.8), channel_id=1, source_target_pairs={{0,48},{2,67},{1,49},{3,2},{64,112},{66,3},{65,113},{67,66},{4,52}... | collective-permute-start | bytes 1572872 | tf_op jit(solution)/shard_map/ppermute | solution.py:37
  76.2 1.5 fusion.62
  78.7 2.8 %collective-permute-start.7 = (bf16[1024,384]{1,0:T(8,128)(2,1)S(1)}, bf16[1024,384]{1,0:T(8,128)(2,1)S(1)}, u32[]{:S(2)}, u32[]{:S(2)}) collective-permute-start(bf16[1024,384]{1,0:T(8,128)(2,1)S(1)} %bitcast.155), channel_id=1, source_target_pairs={{0,1},{2,18},{1,64},{3,19},{64,65},{66,82},{65,0},{67,83},{4,5},{6... | collective-permute-start | bytes 2359304 | tf_op jit(solution)/shard_map/ppermute | solution.py:37
  81.5 1.0 collective-permute-start.8
  82.5 1.4 collective-permute-start.9
  86.0 1.8 fusion.65
  87.9 12.6 %collective-permute-done.29 = bf16[128,2048]{1,0:T(8,128)(2,1)S(1)} collective-permute-done((bf16[128,2048]{1,0:T(8,128)(2,1)S(1)}, bf16[128,2048]{1,0:T(8,128)(2,1)S(1)}, u32[]{:S(2)}, u32[]{:S(2)}) %collective-permute-start.29) | collective-permute-done | bytes 524320 | tf_op jit(solution)/shard_map/ppermute | solution.py:37
  100.5 1.8 collective-permute-start.5
  102.3 7.2 %collective-permute-done.27 = bf16[128,2048]{1,0:T(8,128)(2,1)S(1)} collective-permute-done((bf16[128,2048]{1,0:T(8,128)(2,1)S(1)}, bf16[128,2048]{1,0:T(8,128)(2,1)S(1)}, u32[]{:S(2)}, u32[]{:S(2)}) %collective-permute-start.27) | collective-permute-done | bytes 524320 | tf_op jit(solution)/shard_map/ppermute | solution.py:37
  109.8 3.6 %collective-permute-done.9.refs_3_ = bf16[1024,384]{1,0:T(8,128)(2,1)S(1)} collective-permute-done((bf16[1024,384]{1,0:T(8,128)(2,1)S(1)}, bf16[1024,384]{1,0:T(8,128)(2,1)S(1)}, u32[]{:S(2)}, u32[]{:S(2)}) %collective-permute-start.9) | collective-permute-done | bytes 786464 | tf_op jit(solution)/shard_map/ppermute | solution.py:37
  113.8 1.0 fusion.2
  114.8 1.0 fusion
  118.6 1.0 fusion.4
  119.6 2.8 %collective-permute-done.25 = bf16[128,1024]{1,0:T(8,128)(2,1)S(1)} collective-permute-done((bf16[128,1024]{1,0:T(8,128)(2,1)S(1)}, bf16[128,1024]{1,0:T(8,128)(2,1)S(1)}, u32[]{:S(2)}, u32[]{:S(2)}) %collective-permute-start.25) | collective-permute-done | bytes 262176 | tf_op jit(solution)/shard_map/ppermute | solution.py:37
  122.4 2.6 %collective-permute-done.26 = bf16[128,1024]{1,0:T(8,128)(2,1)S(1)} collective-permute-done((bf16[128,1024]{1,0:T(8,128)(2,1)S(1)}, bf16[128,1024]{1,0:T(8,128)(2,1)S(1)}, u32[]{:S(2)}, u32[]{:S(2)}) %collective-permute-start.26) | collective-permute-done | bytes 262176 | tf_op jit(solution)/shard_map/ppermute | solution.py:37
  125.0 2.7 %collective-permute-done.24 = bf16[128,1024]{1,0:T(8,128)(2,1)S(1)} collective-permute-done((bf16[128,1024]{1,0:T(8,128)(2,1)S(1)}, bf16[128,1024]{1,0:T(8,128)(2,1)S(1)}, u32[]{:S(2)}, u32[]{:S(2)}) %collective-permute-start.24) | collective-permute-done | bytes 262176 | tf_op jit(solution)/shard_map/ppermute | solution.py:37
  128.7 1.2 collective-permute-start.31
  132.1 2.4 %collective-permute-start.11 = (bf16[128,1024]{1,0:T(8,128)(2,1)S(1)}, bf16[128,1024]{1,0:T(8,128)(2,1)S(1)}, u32[]{:S(2)}, u32[]{:S(2)}) collective-permute-start(bf16[128,1024]{1,0:T(8,128)(2,1)S(1)} %pad_maximum_fusion.13), channel_id=1, source_target_pairs={{0,48},{2,67},{1,49},{3,2},{64,112},{66,3},{65,113},{67,66},{4,52}... | collective-permute-start | bytes 786440 | tf_op jit(solution)/shard_map/ppermute | solution.py:37
  135.3 1.8 fusion.64
  137.6 1.4 collective-permute-done.32
  139.6 2.9 %collective-permute-done.31 = bf16[128,2048]{1,0:T(8,128)(2,1)S(1)} collective-permute-done((bf16[128,2048]{1,0:T(8,128)(2,1)S(1)}, bf16[128,2048]{1,0:T(8,128)(2,1)S(1)}, u32[]{:S(2)}, u32[]{:S(2)}) %collective-permute-start.31) | collective-permute-done | bytes 524320 | tf_op jit(solution)/shard_map/ppermute | solution.py:37
  142.5 1.7 collective-permute-start.20
  144.5 1.5 collective-permute-start.18
  146.0 1.9 pad_maximum_fusion.1
  147.9 3.5 %fusion.8 = f32[4,2,64,1536]{3,2,0,1:T(8,128)S(1)} fusion(bf16[1536,2048,1,1]{1,0,2,3:T(8,128)(2,1)S(1)} %bitcast.150, bf16[4,2,64,2048]{3,2,1,0:T(8,128)(2,1)S(1)} %bitcast.157), kind=kOutput, calls=%fused_computation.10 | convolution fusion | flops 3221225472 | bytes 11534336 | tf_op jit(solution)/shard_map/dot_general | solution.py:186
  151.5 2.3 %collective-permute-done.19 = bf16[128,2048]{1,0:T(8,128)(2,1)S(1)} collective-permute-done((bf16[128,2048]{1,0:T(8,128)(2,1)S(1)}, bf16[128,2048]{1,0:T(8,128)(2,1)S(1)}, u32[]{:S(2)}, u32[]{:S(2)}) %collective-permute-start.19) | collective-permute-done | bytes 524320 | tf_op jit(solution)/shard_map/ppermute | solution.py:37
  154.8 1.8 collective-permute-start.33
  156.6 2.2 %collective-permute-done.18 = bf16[128,2048]{1,0:T(8,128)(2,1)S(1)} collective-permute-done((bf16[128,2048]{1,0:T(8,128)(2,1)S(1)}, bf16[128,2048]{1,0:T(8,128)(2,1)S(1)}, u32[]{:S(2)}, u32[]{:S(2)}) %collective-permute-start.18) | collective-permute-done | bytes 524320 | tf_op jit(solution)/shard_map/ppermute | solution.py:37
  159.1 2.5 %collective-permute-done.10 = bf16[128,1024]{1,0:T(8,128)(2,1)S(1)} collective-permute-done((bf16[128,1024]{1,0:T(8,128)(2,1)S(1)}, bf16[128,1024]{1,0:T(8,128)(2,1)S(1)}, u32[]{:S(2)}, u32[]{:S(2)}) %collective-permute-start.10) | collective-permute-done | bytes 262176 | tf_op jit(solution)/shard_map/ppermute | solution.py:37
  162.0 1.8 collective-permute-start.23
  163.8 2.0 collective-permute-start.22
  165.8 2.2 %collective-permute-done.33 = bf16[4,64,1536]{2,1,0:T(8,128)(2,1)S(1)} collective-permute-done((bf16[4,64,1536]{2,1,0:T(8,128)(2,1)S(1)}, bf16[4,64,1536]{2,1,0:T(8,128)(2,1)S(1)}, u32[]{:S(2)}, u32[]{:S(2)}) %collective-permute-start.33) | collective-permute-done | bytes 786464 | tf_op jit(solution)/shard_map/ppermute | solution.py:37
  168.9 4.0 %collective-permute-done.23 = bf16[128,2048]{1,0:T(8,128)(2,1)S(1)} collective-permute-done((bf16[128,2048]{1,0:T(8,128)(2,1)S(1)}, bf16[128,2048]{1,0:T(8,128)(2,1)S(1)}, u32[]{:S(2)}, u32[]{:S(2)}) %collective-permute-start.23) | collective-permute-done | bytes 524320 | tf_op jit(solution)/shard_map/ppermute | solution.py:37
  172.9 5.2 %collective-permute-done.22 = bf16[128,2048]{1,0:T(8,128)(2,1)S(1)} collective-permute-done((bf16[128,2048]{1,0:T(8,128)(2,1)S(1)}, bf16[128,2048]{1,0:T(8,128)(2,1)S(1)}, u32[]{:S(2)}, u32[]{:S(2)}) %collective-permute-start.22) | collective-permute-done | bytes 524320 | tf_op jit(solution)/shard_map/ppermute | solution.py:37
  178.4 1.9 pad_maximum_fusion
  180.3 3.5 %fusion.66 = f32[4,2,64,1536]{3,2,1,0:T(8,128)S(1)} fusion(bf16[4,2,64,2048]{3,2,1,0:T(8,128)(2,1)S(1)} %bitcast.156, bf16[1536,2048,1,1]{1,0,3,2:T(8,128)(2,1)S(1)} %bitcast.151), kind=kOutput, calls=%fused_computation.137 | convolution fusion | flops 3221225472 | bytes 11534336 | tf_op jit(solution)/shard_map/dot_general | solution.py:186
  183.9 1.6 collective-permute-start.35
  185.5 10.4 %collective-permute-done.35 = bf16[4,64,1536]{2,1,0:T(8,128)(2,1)S(1)} collective-permute-done((bf16[4,64,1536]{2,1,0:T(8,128)(2,1)S(1)}, bf16[4,64,1536]{2,1,0:T(8,128)(2,1)S(1)}, u32[]{:S(2)}, u32[]{:S(2)}) %collective-permute-start.35) | collective-permute-done | bytes 786464 | tf_op jit(solution)/shard_map/ppermute | solution.py:37
  197.1 1.1 collective-permute-start.38
  198.2 2.6 %collective-permute-start.37 = (f32[4,64,384]{2,1,0:T(8,128)S(1)}, f32[4,64,384]{2,1,0:T(8,128)S(1)}, u32[]{:S(2)}, u32[]{:S(2)}) collective-permute-start(f32[4,64,384]{2,1,0:T(8,128)S(1)} %get-tuple-element.33), channel_id=1, source_target_pairs={{0,65},{2,50},{1,0},{3,51},{64,1},{66,114},{65,64},{67,115},{4,69}... | collective-permute-start | bytes 1179656 | tf_op jit(solution)/shard_map/ppermute | solution.py:37
  209.0 1.5 collective-permute-done.36
  (90 shorter events, 20.0 us)
Async XLA Ops:
  1.0 18.6 %copy-start.1 = (bf16[384,2048]{1,0:T(8,128)(2,1)S(1)}, bf16[384,2048]{1,0:T(8,128)(2,1)}, u32[]{:S(2)}) copy-start(bf16[384,2048]{1,0:T(8,128)(2,1)} %refs_0_.15) | copy-start | bytes 4718596
  1.1 18.6 %copy-start.2 = (bf16[384,2048]{1,0:T(8,128)(2,1)S(1)}, bf16[384,2048]{1,0:T(8,128)(2,1)}, u32[]{:S(2)}) copy-start(bf16[384,2048]{1,0:T(8,128)(2,1)} %refs_2_.7) | copy-start | bytes 4718596
  2.2 9.7 %collective-permute-start.2 = (bf16[2,256,384]{2,1,0:T(8,128)(2,1)S(1)}, bf16[2,256,384]{2,1,0:T(8,128)(2,1)S(1)}, u32[]{:S(2)}, u32[]{:S(2)}) collective-permute-start(bf16[2,256,384]{2,1,0:T(8,128)(2,1)S(1)} %pad_maximum_fusion.11), channel_id=1, source_target_pairs={{0,64},{2,34},{1,65},{3,35},{64,0},{66,98},{65,1},{67,99},{4,68},{... | collective-permute-start | bytes 1179656 | tf_op jit(solution)/shard_map/ppermute | solution.py:37
  6.2 11.0 %collective-permute-start.1 = (bf16[2,256,384]{2,1,0:T(8,128)(2,1)S(1)}, bf16[2,256,384]{2,1,0:T(8,128)(2,1)S(1)}, u32[]{:S(2)}, u32[]{:S(2)}) collective-permute-start(bf16[2,256,384]{2,1,0:T(8,128)(2,1)S(1)} %pad_maximum_fusion.11), channel_id=1, source_target_pairs={{0,65},{2,50},{1,0},{3,51},{64,1},{66,114},{65,64},{67,115},{4,69}... | collective-permute-start | bytes 1179656 | tf_op jit(solution)/shard_map/ppermute | solution.py:37
  6.9 10.3 %collective-permute-start = (bf16[2,256,384]{2,1,0:T(8,128)(2,1)S(1)}, bf16[2,256,384]{2,1,0:T(8,128)(2,1)S(1)}, u32[]{:S(2)}, u32[]{:S(2)}) collective-permute-start(bf16[2,256,384]{2,1,0:T(8,128)(2,1)S(1)} %pad_maximum_fusion.11), channel_id=1, source_target_pairs={{0,1},{2,18},{1,64},{3,19},{64,65},{66,82},{65,0},{67,83},{4,5},{6... | collective-permute-start | bytes 1179656 | tf_op jit(solution)/shard_map/ppermute | solution.py:37
  8.2 11.5 %collective-permute-start.13 = (bf16[384,2048]{1,0:T(8,128)(2,1)}, bf16[384,2048]{1,0:T(8,128)(2,1)}, u32[]{:S(2)}, u32[]{:S(2)}) collective-permute-start(bf16[384,2048]{1,0:T(8,128)(2,1)} %refs_0_.15), channel_id=1, source_target_pairs={{0,2},{2,0},{1,3},{3,1},{64,66},{66,64},{65,67},{67,65},{4,6},{6,4... | collective-permute-start | bytes 4718600 | tf_op jit(solution)/shard_map/ppermute | solution.py:37
  8.2 11.5 %collective-permute-start.14 = (bf16[384,2048]{1,0:T(8,128)(2,1)}, bf16[384,2048]{1,0:T(8,128)(2,1)}, u32[]{:S(2)}, u32[]{:S(2)}) collective-permute-start(bf16[384,2048]{1,0:T(8,128)(2,1)} %refs_2_.7), channel_id=1, source_target_pairs={{0,2},{2,0},{1,3},{3,1},{64,66},{66,64},{65,67},{67,65},{4,6},{6,4... | collective-permute-start | bytes 4718600 | tf_op jit(solution)/shard_map/ppermute | solution.py:37
  19.4 20.7 %collective-permute-start.3 = (bf16[2,256,1536]{2,1,0:T(8,128)(2,1)}, bf16[2,256,1536]{2,1,0:T(8,128)(2,1)}, u32[]{:S(2)}, u32[]{:S(2)}) collective-permute-start(bf16[2,256,1536]{2,1,0:T(8,128)(2,1)} %pad_maximum_fusion.2), channel_id=1, source_target_pairs={{0,4},{2,14},{1,5},{3,15},{64,68},{66,78},{65,69},{67,79},{4,8},{6... | collective-permute-start | bytes 4718600 | tf_op jit(solution)/shard_map/ppermute | solution.py:37
  23.0 23.6 %collective-permute-start.15 = (bf16[384,2048]{1,0:T(8,128)(2,1)}, bf16[384,2048]{1,0:T(8,128)(2,1)}, u32[]{:S(2)}, u32[]{:S(2)}) collective-permute-start(bf16[384,2048]{1,0:T(8,128)(2,1)} %shard_map.70), channel_id=1, source_target_pairs={{0,1},{2,18},{1,64},{3,19},{64,65},{66,82},{65,0},{67,83},{4,5},{6... | collective-permute-start | bytes 4718600 | tf_op jit(solution)/shard_map/ppermute | solution.py:37
  24.0 5.6 %copy-start.3 = (bf16[384,2048]{1,0:T(8,128)(2,1)S(1)}, bf16[384,2048]{1,0:T(8,128)(2,1)}, u32[]{:S(2)}) copy-start(bf16[384,2048]{1,0:T(8,128)(2,1)} %refs_2_.7) | copy-start | bytes 4718596
  27.3 37.4 %collective-permute-start.16 = (bf16[384,2048]{1,0:T(8,128)(2,1)}, bf16[384,2048]{1,0:T(8,128)(2,1)}, u32[]{:S(2)}, u32[]{:S(2)}) collective-permute-start(bf16[384,2048]{1,0:T(8,128)(2,1)} %shard_map.71), channel_id=1, source_target_pairs={{0,65},{2,50},{1,0},{3,51},{64,1},{66,114},{65,64},{67,115},{4,69}... | collective-permute-start | bytes 4718600 | tf_op jit(solution)/shard_map/ppermute | solution.py:37
  29.5 12.1 %copy-start = (bf16[2048,384]{1,0:T(8,128)(2,1)S(1)}, bf16[2048,384]{1,0:T(8,128)(2,1)}, u32[]{:S(2)}) copy-start(bf16[2048,384]{1,0:T(8,128)(2,1)} %refs_0_.11) | copy-start | bytes 4718596
  32.9 31.8 %collective-permute-start.17 = (bf16[384,2048]{1,0:T(8,128)(2,1)}, bf16[384,2048]{1,0:T(8,128)(2,1)}, u32[]{:S(2)}, u32[]{:S(2)}) collective-permute-start(bf16[384,2048]{1,0:T(8,128)(2,1)} %shard_map.72), channel_id=1, source_target_pairs={{0,64},{2,34},{1,65},{3,35},{64,0},{66,98},{65,1},{67,99},{4,68},{... | collective-permute-start | bytes 4718600 | tf_op jit(solution)/shard_map/ppermute | solution.py:37
  40.2 29.7 %collective-permute-start.4 = (bf16[2,256,1536]{2,1,0:T(8,128)(2,1)}, bf16[2,256,1536]{2,1,0:T(8,128)(2,1)}, u32[]{:S(2)}, u32[]{:S(2)}) collective-permute-start(bf16[2,256,1536]{2,1,0:T(8,128)(2,1)} %collective-permute-done.3), channel_id=1, source_target_pairs={{0,4},{2,14},{1,5},{3,15},{64,68},{66,78},{65,69},{67,79},{4,8},{6... | collective-permute-start | bytes 4718600 | tf_op jit(solution)/shard_map/ppermute | solution.py:37
  41.6 36.1 %collective-permute-start.6 = (bf16[2048,384]{1,0:T(8,128)(2,1)S(1)}, bf16[2048,384]{1,0:T(8,128)(2,1)S(1)}, u32[]{:S(2)}, u32[]{:S(2)}) collective-permute-start(bf16[2048,384]{1,0:T(8,128)(2,1)S(1)} %copy-done), channel_id=1, source_target_pairs={{0,2},{2,0},{1,3},{3,1},{64,66},{66,64},{65,67},{67,65},{4,6},{6,4... | collective-permute-start | bytes 4718600 | tf_op jit(solution)/shard_map/ppermute | solution.py:37
  41.6 1.4 copy-start.4
  73.4 11.9 %collective-permute-start.28 = (bf16[128,2048]{1,0:T(8,128)(2,1)S(1)}, bf16[128,2048]{1,0:T(8,128)(2,1)S(1)}, u32[]{:S(2)}, u32[]{:S(2)}) collective-permute-start(bf16[128,2048]{1,0:T(8,128)(2,1)S(1)} %pad_maximum_fusion.8), channel_id=1, source_target_pairs={{0,48},{2,67},{1,49},{3,2},{64,112},{66,3},{65,113},{67,66},{4,52}... | collective-permute-start | bytes 1572872 | tf_op jit(solution)/shard_map/ppermute | solution.py:37
  78.7 31.1 %collective-permute-start.7 = (bf16[1024,384]{1,0:T(8,128)(2,1)S(1)}, bf16[1024,384]{1,0:T(8,128)(2,1)S(1)}, u32[]{:S(2)}, u32[]{:S(2)}) collective-permute-start(bf16[1024,384]{1,0:T(8,128)(2,1)S(1)} %bitcast.155), channel_id=1, source_target_pairs={{0,1},{2,18},{1,64},{3,19},{64,65},{66,82},{65,0},{67,83},{4,5},{6... | collective-permute-start | bytes 2359304 | tf_op jit(solution)/shard_map/ppermute | solution.py:37
  81.5 28.3 %collective-permute-start.8 = (bf16[1024,384]{1,0:T(8,128)(2,1)S(1)}, bf16[1024,384]{1,0:T(8,128)(2,1)S(1)}, u32[]{:S(2)}, u32[]{:S(2)}) collective-permute-start(bf16[1024,384]{1,0:T(8,128)(2,1)S(1)} %bitcast.154), channel_id=1, source_target_pairs={{0,65},{2,50},{1,0},{3,51},{64,1},{66,114},{65,64},{67,115},{4,69}... | collective-permute-start | bytes 2359304 | tf_op jit(solution)/shard_map/ppermute | solution.py:37
  82.5 30.9 %collective-permute-start.9 = (bf16[1024,384]{1,0:T(8,128)(2,1)S(1)}, bf16[1024,384]{1,0:T(8,128)(2,1)S(1)}, u32[]{:S(2)}, u32[]{:S(2)}) collective-permute-start(bf16[1024,384]{1,0:T(8,128)(2,1)S(1)} %bitcast.153), channel_id=1, source_target_pairs={{0,64},{2,34},{1,65},{3,35},{64,0},{66,98},{65,1},{67,99},{4,68},{... | collective-permute-start | bytes 2359304 | tf_op jit(solution)/shard_map/ppermute | solution.py:37
  83.9 16.5 %collective-permute-start.29 = (bf16[128,2048]{1,0:T(8,128)(2,1)S(1)}, bf16[128,2048]{1,0:T(8,128)(2,1)S(1)}, u32[]{:S(2)}, u32[]{:S(2)}) collective-permute-start(bf16[128,2048]{1,0:T(8,128)(2,1)S(1)} %pad_maximum_fusion.9), channel_id=1, source_target_pairs={{0,32},{2,66},{1,33},{3,67},{64,96},{66,2},{65,97},{67,3},{4,36},{... | collective-permute-start | bytes 1572872 | tf_op jit(solution)/shard_map/ppermute | solution.py:37
  85.3 24.2 %collective-permute-start.27 = (bf16[128,2048]{1,0:T(8,128)(2,1)S(1)}, bf16[128,2048]{1,0:T(8,128)(2,1)S(1)}, u32[]{:S(2)}, u32[]{:S(2)}) collective-permute-start(bf16[128,2048]{1,0:T(8,128)(2,1)S(1)} %pad_maximum_fusion.7), channel_id=1, source_target_pairs={{0,16},{2,3},{1,17},{3,66},{64,80},{66,67},{65,81},{67,2},{4,20},{... | collective-permute-start | bytes 1572872 | tf_op jit(solution)/shard_map/ppermute | solution.py:37
  100.5 30.3 %collective-permute-start.5 = (bf16[2,256,1536]{2,1,0:T(8,128)(2,1)}, bf16[2,256,1536]{2,1,0:T(8,128)(2,1)S(1)}, u32[]{:S(2)}, u32[]{:S(2)}) collective-permute-start(bf16[2,256,1536]{2,1,0:T(8,128)(2,1)} %pad_maximum_fusion.2), channel_id=1, source_target_pairs={{0,12},{2,6},{1,13},{3,7},{64,76},{66,70},{65,77},{67,71},{4,0},{6... | collective-permute-start | bytes 4718600 | tf_op jit(solution)/shard_map/ppermute | solution.py:37
  116.0 6.4 %collective-permute-start.25 = (bf16[128,1024]{1,0:T(8,128)(2,1)S(1)}, bf16[128,1024]{1,0:T(8,128)(2,1)S(1)}, u32[]{:S(2)}, u32[]{:S(2)}) collective-permute-start(bf16[128,1024]{1,0:T(8,128)(2,1)S(1)} %pad_maximum_fusion.16), channel_id=1, source_target_pairs={{0,48},{2,67},{1,49},{3,2},{64,112},{66,3},{65,113},{67,66},{4,52}... | collective-permute-start | bytes 786440 | tf_op jit(solution)/shard_map/ppermute | solution.py:37
  117.0 8.1 %collective-permute-start.26 = (bf16[128,1024]{1,0:T(8,128)(2,1)S(1)}, bf16[128,1024]{1,0:T(8,128)(2,1)S(1)}, u32[]{:S(2)}, u32[]{:S(2)}) collective-permute-start(bf16[128,1024]{1,0:T(8,128)(2,1)S(1)} %pad_maximum_fusion.17), channel_id=1, source_target_pairs={{0,32},{2,66},{1,33},{3,67},{64,96},{66,2},{65,97},{67,3},{4,36},{... | collective-permute-start | bytes 786440 | tf_op jit(solution)/shard_map/ppermute | solution.py:37
  117.6 10.2 %collective-permute-start.24 = (bf16[128,1024]{1,0:T(8,128)(2,1)S(1)}, bf16[128,1024]{1,0:T(8,128)(2,1)S(1)}, u32[]{:S(2)}, u32[]{:S(2)}) collective-permute-start(bf16[128,1024]{1,0:T(8,128)(2,1)S(1)} %pad_maximum_fusion.15), channel_id=1, source_target_pairs={{0,16},{2,3},{1,17},{3,66},{64,80},{66,67},{65,81},{67,2},{4,20},{... | collective-permute-start | bytes 786440 | tf_op jit(solution)/shard_map/ppermute | solution.py:37
  128.1 10.9 %collective-permute-start.32 = (bf16[128,2048]{1,0:T(8,128)(2,1)S(1)}, bf16[128,2048]{1,0:T(8,128)(2,1)S(1)}, u32[]{:S(2)}, u32[]{:S(2)}) collective-permute-start(bf16[128,2048]{1,0:T(8,128)(2,1)S(1)} %pad_maximum_fusion.10), channel_id=1, source_target_pairs={{0,32},{2,66},{1,33},{3,67},{64,96},{66,2},{65,97},{67,3},{4,36},{... | collective-permute-start | bytes 1572872 | tf_op jit(solution)/shard_map/ppermute | solution.py:37
  128.7 13.8 %collective-permute-start.31 = (bf16[128,2048]{1,0:T(8,128)(2,1)S(1)}, bf16[128,2048]{1,0:T(8,128)(2,1)S(1)}, u32[]{:S(2)}, u32[]{:S(2)}) collective-permute-start(bf16[128,2048]{1,0:T(8,128)(2,1)S(1)} %pad_maximum_fusion.10), channel_id=1, source_target_pairs={{0,48},{2,67},{1,49},{3,2},{64,112},{66,3},{65,113},{67,66},{4,52}... | collective-permute-start | bytes 1572872 | tf_op jit(solution)/shard_map/ppermute | solution.py:37
  129.9 14.6 %collective-permute-start.30 = (bf16[128,2048]{1,0:T(8,128)(2,1)S(1)}, bf16[128,2048]{1,0:T(8,128)(2,1)S(1)}, u32[]{:S(2)}, u32[]{:S(2)}) collective-permute-start(bf16[128,2048]{1,0:T(8,128)(2,1)S(1)} %pad_maximum_fusion.10), channel_id=1, source_target_pairs={{0,16},{2,3},{1,17},{3,66},{64,80},{66,67},{65,81},{67,2},{4,20},{... | collective-permute-start | bytes 1572872 | tf_op jit(solution)/shard_map/ppermute | solution.py:37
  132.1 27.0 %collective-permute-start.11 = (bf16[128,1024]{1,0:T(8,128)(2,1)S(1)}, bf16[128,1024]{1,0:T(8,128)(2,1)S(1)}, u32[]{:S(2)}, u32[]{:S(2)}) collective-permute-start(bf16[128,1024]{1,0:T(8,128)(2,1)S(1)} %pad_maximum_fusion.13), channel_id=1, source_target_pairs={{0,48},{2,67},{1,49},{3,2},{64,112},{66,3},{65,113},{67,66},{4,52}... | collective-permute-start | bytes 786440 | tf_op jit(solution)/shard_map/ppermute | solution.py:37
  134.6 24.6 %collective-permute-start.12 = (bf16[128,1024]{1,0:T(8,128)(2,1)S(1)}, bf16[128,1024]{1,0:T(8,128)(2,1)S(1)}, u32[]{:S(2)}, u32[]{:S(2)}) collective-permute-start(bf16[128,1024]{1,0:T(8,128)(2,1)S(1)} %pad_maximum_fusion.14), channel_id=1, source_target_pairs={{0,32},{2,66},{1,33},{3,67},{64,96},{66,2},{65,97},{67,3},{4,36},{... | collective-permute-start | bytes 786440 | tf_op jit(solution)/shard_map/ppermute | solution.py:37
  139.0 14.8 %collective-permute-start.19 = (bf16[128,2048]{1,0:T(8,128)(2,1)S(1)}, bf16[128,2048]{1,0:T(8,128)(2,1)S(1)}, u32[]{:S(2)}, u32[]{:S(2)}) collective-permute-start(bf16[128,2048]{1,0:T(8,128)(2,1)S(1)} %pad_maximum_fusion.4), channel_id=1, source_target_pairs={{0,48},{2,67},{1,49},{3,2},{64,112},{66,3},{65,113},{67,66},{4,52}... | collective-permute-start | bytes 1572872 | tf_op jit(solution)/shard_map/ppermute | solution.py:37
  142.5 12.3 %collective-permute-start.20 = (bf16[128,2048]{1,0:T(8,128)(2,1)S(1)}, bf16[128,2048]{1,0:T(8,128)(2,1)S(1)}, u32[]{:S(2)}, u32[]{:S(2)}) collective-permute-start(bf16[128,2048]{1,0:T(8,128)(2,1)S(1)} %pad_maximum_fusion.5), channel_id=1, source_target_pairs={{0,32},{2,66},{1,33},{3,67},{64,96},{66,2},{65,97},{67,3},{4,36},{... | collective-permute-start | bytes 1572872 | tf_op jit(solution)/shard_map/ppermute | solution.py:37
  144.5 14.3 %collective-permute-start.18 = (bf16[128,2048]{1,0:T(8,128)(2,1)S(1)}, bf16[128,2048]{1,0:T(8,128)(2,1)S(1)}, u32[]{:S(2)}, u32[]{:S(2)}) collective-permute-start(bf16[128,2048]{1,0:T(8,128)(2,1)S(1)} %pad_maximum_fusion.3), channel_id=1, source_target_pairs={{0,16},{2,3},{1,17},{3,66},{64,80},{66,67},{65,81},{67,2},{4,20},{... | collective-permute-start | bytes 1572872 | tf_op jit(solution)/shard_map/ppermute | solution.py:37
  153.8 7.8 %collective-permute-start.10 = (bf16[128,1024]{1,0:T(8,128)(2,1)S(1)}, bf16[128,1024]{1,0:T(8,128)(2,1)S(1)}, u32[]{:S(2)}, u32[]{:S(2)}) collective-permute-start(bf16[128,1024]{1,0:T(8,128)(2,1)S(1)} %pad_maximum_fusion.12), channel_id=1, source_target_pairs={{0,16},{2,3},{1,17},{3,66},{64,80},{66,67},{65,81},{67,2},{4,20},{... | collective-permute-start | bytes 786440 | tf_op jit(solution)/shard_map/ppermute | solution.py:37
  154.8 13.2 %collective-permute-start.33 = (bf16[4,64,1536]{2,1,0:T(8,128)(2,1)S(1)}, bf16[4,64,1536]{2,1,0:T(8,128)(2,1)S(1)}, u32[]{:S(2)}, u32[]{:S(2)}) collective-permute-start(bf16[4,64,1536]{2,1,0:T(8,128)(2,1)S(1)} %fusion.18), channel_id=1, source_target_pairs={{0,12},{2,6},{1,13},{3,7},{64,76},{66,70},{65,77},{67,71},{4,0},{6... | collective-permute-start | bytes 2359304 | tf_op jit(solution)/shard_map/ppermute | solution.py:37
  162.0 10.9 %collective-permute-start.23 = (bf16[128,2048]{1,0:T(8,128)(2,1)S(1)}, bf16[128,2048]{1,0:T(8,128)(2,1)S(1)}, u32[]{:S(2)}, u32[]{:S(2)}) collective-permute-start(bf16[128,2048]{1,0:T(8,128)(2,1)S(1)} %pad_maximum_fusion.6), channel_id=1, source_target_pairs={{0,32},{2,66},{1,33},{3,67},{64,96},{66,2},{65,97},{67,3},{4,36},{... | collective-permute-start | bytes 1572872 | tf_op jit(solution)/shard_map/ppermute | solution.py:37
  163.8 14.3 %collective-permute-start.22 = (bf16[128,2048]{1,0:T(8,128)(2,1)S(1)}, bf16[128,2048]{1,0:T(8,128)(2,1)S(1)}, u32[]{:S(2)}, u32[]{:S(2)}) collective-permute-start(bf16[128,2048]{1,0:T(8,128)(2,1)S(1)} %pad_maximum_fusion.6), channel_id=1, source_target_pairs={{0,48},{2,67},{1,49},{3,2},{64,112},{66,3},{65,113},{67,66},{4,52}... | collective-permute-start | bytes 1572872 | tf_op jit(solution)/shard_map/ppermute | solution.py:37
  165.8 12.6 %collective-permute-start.21 = (bf16[128,2048]{1,0:T(8,128)(2,1)S(1)}, bf16[128,2048]{1,0:T(8,128)(2,1)S(1)}, u32[]{:S(2)}, u32[]{:S(2)}) collective-permute-start(bf16[128,2048]{1,0:T(8,128)(2,1)S(1)} %pad_maximum_fusion.6), channel_id=1, source_target_pairs={{0,16},{2,3},{1,17},{3,66},{64,80},{66,67},{65,81},{67,2},{4,20},{... | collective-permute-start | bytes 1572872 | tf_op jit(solution)/shard_map/ppermute | solution.py:37
  168.2 17.3 %collective-permute-start.34 = (bf16[4,64,1536]{2,1,0:T(8,128)(2,1)S(1)}, bf16[4,64,1536]{2,1,0:T(8,128)(2,1)S(1)}, u32[]{:S(2)}, u32[]{:S(2)}) collective-permute-start(bf16[4,64,1536]{2,1,0:T(8,128)(2,1)S(1)} %fusion.11), channel_id=1, source_target_pairs={{0,12},{2,6},{1,13},{3,7},{64,76},{66,70},{65,77},{67,71},{4,0},{6... | collective-permute-start | bytes 2359304 | tf_op jit(solution)/shard_map/ppermute | solution.py:37
  183.9 12.1 %collective-permute-start.35 = (bf16[4,64,1536]{2,1,0:T(8,128)(2,1)S(1)}, bf16[4,64,1536]{2,1,0:T(8,128)(2,1)S(1)}, u32[]{:S(2)}, u32[]{:S(2)}) collective-permute-start(bf16[4,64,1536]{2,1,0:T(8,128)(2,1)S(1)} %fusion.19), channel_id=1, source_target_pairs={{0,4},{2,14},{1,5},{3,15},{64,68},{66,78},{65,69},{67,79},{4,8},{6... | collective-permute-start | bytes 2359304 | tf_op jit(solution)/shard_map/ppermute | solution.py:37
  196.2 4.6 %copy-start.5 = (s32[4]{0:T(128)S(1)}, s32[4]{0:T(128)}, u32[]{:S(2)}) copy-start(s32[4]{0:T(128)} %constant.251.clone) | copy-start | bytes 52
  197.1 13.4 %collective-permute-start.36 = (f32[4,64,384]{2,1,0:T(8,128)}, f32[4,64,384]{2,1,0:T(8,128)S(1)}, u32[]{:S(2)}, u32[]{:S(2)}) collective-permute-start(f32[4,64,384]{2,1,0:T(8,128)} %get-tuple-element.31), channel_id=1, source_target_pairs={{0,1},{2,18},{1,64},{3,19},{64,65},{66,82},{65,0},{67,83},{4,5},{6... | collective-permute-start | bytes 1179656 | tf_op jit(solution)/shard_map/ppermute | solution.py:37
  197.1 13.4 %collective-permute-start.38 = (f32[4,64,384]{2,1,0:T(8,128)S(1)}, f32[4,64,384]{2,1,0:T(8,128)S(1)}, u32[]{:S(2)}, u32[]{:S(2)}) collective-permute-start(f32[4,64,384]{2,1,0:T(8,128)S(1)} %get-tuple-element.32), channel_id=1, source_target_pairs={{0,64},{2,34},{1,65},{3,35},{64,0},{66,98},{65,1},{67,99},{4,68},{... | collective-permute-start | bytes 1179656 | tf_op jit(solution)/shard_map/ppermute | solution.py:37
  198.2 13.0 %collective-permute-start.37 = (f32[4,64,384]{2,1,0:T(8,128)S(1)}, f32[4,64,384]{2,1,0:T(8,128)S(1)}, u32[]{:S(2)}, u32[]{:S(2)}) collective-permute-start(f32[4,64,384]{2,1,0:T(8,128)S(1)} %get-tuple-element.33), channel_id=1, source_target_pairs={{0,65},{2,50},{1,0},{3,51},{64,1},{66,114},{65,64},{67,115},{4,69}... | collective-permute-start | bytes 1179656 | tf_op jit(solution)/shard_map/ppermute | solution.py:37
